TPU v7x, 32 devices: a whole 2x2x4 slice. The times are simulated.
32 devices in a mesh: row: 8 (over z, y), col: 4 (over x, core).
Axes of the slice: x: 2, y: 2, z: 4, core: 2. Of those that a mesh axis runs over, the one named last changes fastest.
Arguments:
- rhs: float32 [32, 65536], P(None, ('row', 'col')), may hold values from -5 to 7
- coords: float32 [3, 65536], P(None, ('row', 'col')), may hold values from 0 to 8, as said below
- nugget: float32 [65536], P(('row', 'col')), may hold values from 1.5 to 3
- near_ids: int32 [128, 3], P(('row', 'col')), may hold values from -1 to 127, as said below
- basis: float32 [7, 128, 65536], P(None, None, ('row', 'col')), may hold values from -6 to 6
Outputs:
- solution: float32 [32, 65536], P(None, ('row', 'col'))
- residual: float32 [32, 65536], P(None, ('row', 'col'))
Inputs may be any that keep to these rules, and one draw needn't show every extreme that they name: `near_ids`: row i lists leaf i and some of the leaves i - 1 to i + 1 inside the range, each at most once, in any order; the other slots hold -1; the first and last leaf of each device's block of 4 list all such leaves inside the range. `coords`: each leaf's points lie in a unit box with an integer corner; consecutive leaves lie in boxes that share a face.
All inputs are finite; a program needn't handle non-finite values.
Results may differ from a plain program's by a relative error of at most 0.0003.
Values sent between devices are 32-bit elements; how exact they have to be, the bound alone decides.
No kernel may reach another device: no remote copies, remote signals or barrier semaphores. Data moves between devices by JAX's collectives and lax.ppermute only.
A program may use at most 128 MiB of HBM per device.

v0:
```python
import functools

import jax
import jax.numpy as jnp
from jax import lax
from jax.experimental import pallas as pl
from jax.experimental.pallas import tpu as pltpu
from jax.sharding import PartitionSpec as P

LEAF = 512
ITERS = 4
WIN = 3
LANES = 128
LOCAL = 3
SPARE = 8
CHUNK = 16
NORM_TILE = 8
PRODUCTS_TILE = 8
FLOPS = 3 * 10**9

root_three = 1.7320508075688772
spacing_factor = 1.6
matern_scale = root_three / (spacing_factor * LEAF ** (-1.0 / 3.0))

BOTH = ("row", "col")
ROWS_COLS = (((1,), (0,)), ((), ()))
ROWS_ROWS = (((1,), (1,)), ((), ()))

PAIRS = ("dq", "rq", "qq", "rw", "dw", "rz", "qz", "dz")


def halves(values):
    high = values.astype(jnp.bfloat16)
    low = (values - high.astype(jnp.float32)).astype(jnp.bfloat16)
    return high, low


def stacked(values):
    return jnp.concatenate(halves(values), axis=0)


def product(stack, high, low, dims):
    rows = stack.shape[0] // 2
    main = lax.dot_general(stack, high, dims, preferred_element_type=jnp.float32)
    rest = lax.dot_general(stack[:rows], low, dims, preferred_element_type=jnp.float32)
    return main[:rows] + (main[rows:] + rest)


def row_sum(values):
    return jnp.sum(values, axis=1, keepdims=True)


def in_lanes(columns, shape):
    lane = lax.broadcasted_iota(jnp.int32, shape, 1)
    block = jnp.zeros(shape, jnp.float32)
    for index, column in enumerate(columns):
        block = jnp.where(lane == index, column, block)
    return block


def sums_tile(columns, rows, depth):
    turned = in_lanes(columns, (rows, LANES)).T[:depth]
    return jnp.concatenate([turned, jnp.zeros((depth, LANES - rows), jnp.float32)], axis=1)


def level_terms(core, columns, rows, depth):
    twice = [jnp.concatenate([column, column], axis=0) for column in columns]
    zero = jnp.zeros((rows, 1), jnp.float32)
    tile = sums_tile([zero] * (len(PAIRS) - len(columns)) + twice, rows, depth)
    lane = lax.broadcasted_iota(jnp.int32, tile.shape, 1)
    return jnp.where(lane // (rows // 2) == core, tile, 0.0)


def chosen(core, odd, even):
    return jnp.where(core == 1, odd, even)


def whole(memory=pltpu.VMEM):
    return pl.BlockSpec(memory_space=memory)


def call(body, outs, *args, scalars=0, flops=0, traffic=2**20, limit=16, scratch=()):
    return pl.pallas_call(
        body,
        out_shape=outs,
        in_specs=[whole(pltpu.SMEM)] * scalars + [whole()] * (len(args) - scalars),
        out_specs=[whole()] * len(outs),
        scratch_shapes=scratch,
        compiler_params=pltpu.CompilerParams(vmem_limit_bytes=limit * 2**20),
        cost_estimate=pl.CostEstimate(flops=flops, bytes_accessed=traffic, transcendentals=0),
    )(*args)


def f32(*shape):
    return jax.ShapeDtypeStruct(shape, jnp.float32)


def bf16(*shape):
    return jax.ShapeDtypeStruct(shape, jnp.bfloat16)


def matrix_rows(rows, lanes):
    square = None
    for axis in range(3):
        spread = rows[:, axis : axis + 1] - lanes[axis : axis + 1]
        square = spread * spread if square is None else square + spread * spread
    scaled = square * lax.rsqrt(jnp.maximum(square, 1e-30))
    return halves((1.0 + scaled) * jnp.exp(-scaled))


def fill_matrices(groups, lane_ref, sub_ref, high_ref, low_ref):
    sub_ref[...] = lane_ref[...].T
    matrix = 0
    for row_leaf, col_leaves in groups:
        lanes = [lane_ref[:, leaf * LEAF : (leaf + 1) * LEAF] for leaf in col_leaves]

        def one(part, carry):
            row_at = pl.multiple_of(row_leaf * LEAF + part * CHUNK, CHUNK)
            out_at = pl.ds(pl.multiple_of(part * CHUNK, CHUNK), CHUNK)
            rows = sub_ref[pl.ds(row_at, CHUNK)]
            for index, far in enumerate(lanes):
                values = matrix_rows(rows, far)
                high_ref[matrix + index, out_at], low_ref[matrix + index, out_at] = values
            return carry

        lax.fori_loop(0, LEAF // CHUNK, one, 0, unroll=4)
        matrix += len(col_leaves)


def setup_kernel(groups, coords_ref, basis_ref, high_ref, low_ref, basis_high_ref, basis_low_ref, lane_ref, *scratch):
    sub_ref, raw_ref, sem_ref = scratch
    levels, rank, _ = basis_ref.shape
    copies = [pltpu.make_async_copy(basis_ref.at[at], raw_ref.at[at], sem_ref.at[at]) for at in range(levels)]
    for copy in copies:
        copy.start()
    scaled = coords_ref[...] * matern_scale
    lane_ref[...] = jnp.concatenate([scaled, jnp.zeros((8 - scaled.shape[0], scaled.shape[1]), jnp.float32)], axis=0)
    fill_matrices(groups, lane_ref, sub_ref, high_ref, low_ref)
    for at, copy in enumerate(copies):
        copy.wait()
        here = slice(at * rank, (at + 1) * rank)
        basis_high_ref[here], basis_low_ref[here] = halves(raw_ref[at])


def edge_matrices(core_ref, rows, lane_ref, paired_ref, other_ref, high_ref, low_ref, sub_ref):
    core = core_ref[0]
    leaves = lane_ref.shape[1] // LEAF
    sub_ref[...] = lane_ref[...].T
    paired = paired_ref[rows : rows + 3]
    other = other_ref[rows : rows + 3]
    lanes = [chosen(core, paired, other), chosen(core, other, paired)]

    for side in range(2):
        first_row = side * (leaves - 1) * LEAF

        def one(part, carry):
            row_at = pl.multiple_of(first_row + part * CHUNK, CHUNK)
            out_at = pl.ds(pl.multiple_of(part * CHUNK, CHUNK), CHUNK)
            values = matrix_rows(sub_ref[pl.ds(row_at, CHUNK)], lanes[side])
            high_ref[side, out_at], low_ref[side, out_at] = values
            return carry

        lax.fori_loop(0, LEAF // CHUNK, one, 0, unroll=4)


def sides(core, field_ref):
    head = field_ref[:, :LEAF]
    tail = field_ref[:, field_ref.shape[1] - LEAF :]
    return chosen(core, head, tail), chosen(core, tail, head)


def edges_kernel(core_ref, field_ref, lane_ref, paired_ref, other_ref):
    core = core_ref[0]
    for ref, field, place in zip((paired_ref, other_ref), sides(core, field_ref), sides(core, lane_ref)):
        ref[...] = jnp.concatenate([field, place], axis=0)


def down_kernel(core_ref, field_ref, high_ref, low_ref, local_ref, keep_ref, send_ref, *tile_refs):
    core = core_ref[0]
    rank = LANES
    rows, width = field_ref.shape
    half = width // 2
    stack = stacked(field_ref[...])
    for part in range(2):
        points = slice(part * half, (part + 1) * half)
        local_ref[:, part * rank : (part + 1) * rank] = product(
            stack[:, points], high_ref[:rank, points], low_ref[:rank, points], ROWS_ROWS
        )
    all_points = product(stack, high_ref[rank:], low_ref[rank:], ROWS_ROWS)
    local_ref[:, 2 * rank :] = all_points[:, :rank]
    own = rows // 2
    for bit in range(all_points.shape[1] // rank - 1):
        block = all_points[:, (bit + 1) * rank : (bit + 2) * rank]
        keep_ref[bit * own : (bit + 1) * own] = chosen(core, block[own:], block[:own])
        send_ref[bit * own : (bit + 1) * own] = chosen(core, block[:own], block[own:])
    for ref in tile_refs:
        ref[...] = sums_tile([row_sum(field_ref[...] * field_ref[...])], rows, NORM_TILE)


def leaf_of(ref, leaf):
    return ref[:, leaf * LEAF : (leaf + 1) * LEAF]


def weight_of(weights_ref, leaf, offset):
    at = WIN * leaf + offset + 1
    return weights_ref[at : at + 1]


def leaf_weights(near_ids, first_leaf):
    target = first_leaf + jnp.arange(near_ids.shape[0])[:, None] + jnp.arange(WIN)[None, :] - 1
    found = jnp.any(near_ids[:, None, :] == target[:, :, None], axis=2) & (target >= 0)
    weights = jnp.where(found, 1.0 / (16 * WIN), 0.0).astype(jnp.float32)
    return jnp.broadcast_to(weights.reshape(-1, 1), (weights.size, LEAF))


def row_groups(leaves):
    return [(leaf, [leaf, leaf + 1] if leaf + 1 < leaves else [leaf]) for leaf in range(leaves)]


def inner_kernel(half, weights_ref, field_ref, nugget_ref, *refs):
    out_ref = refs[-1]
    leaves = weights_ref.shape[0] // WIN
    start = half * (leaves // 2)
    stop = start + leaves // 2
    pieces = {leaf: stacked(leaf_of(field_ref, leaf)) for leaf in range(max(start - 1, 0), min(stop + 1, leaves))}
    pairs = [(row, col) for row, cols in row_groups(leaves) for col in cols]

    def matrix(row, col):
        at = pairs.index((row, col))
        front = refs[0].shape[0]
        return (refs[0][at], refs[1][at]) if at < front else (refs[2][at - front], refs[3][at - front])

    for leaf in range(start, stop):
        at = leaf - start
        inside = product(pieces[leaf], *matrix(leaf, leaf), ROWS_COLS)
        total = leaf_of(nugget_ref, leaf) * leaf_of(field_ref, leaf) + weight_of(weights_ref, leaf, 0) * inside
        if leaf > 0:
            before = product(pieces[leaf - 1], *matrix(leaf - 1, leaf), ROWS_COLS)
            total = total + weight_of(weights_ref, leaf, -1) * before
        if leaf < leaves - 1:
            after = product(pieces[leaf + 1], *matrix(leaf, leaf + 1), ROWS_ROWS)
            total = total + weight_of(weights_ref, leaf, 1) * after
        out_ref[:, at * LEAF : (at + 1) * LEAF] = total


def edge_kernel(sums, *refs):
    core_ref, weights_ref, paired_ref, other_ref, high_ref, low_ref, front_ref, back_ref = refs[:8]
    refs = refs[8:]
    out_ref = refs[-2] if sums else refs[-1]
    core = core_ref[0]
    rows, width = out_ref.shape
    leaves = width // LEAF
    before = chosen(core, paired_ref[:rows], other_ref[:rows])
    after = chosen(core, other_ref[:rows], paired_ref[:rows])
    out_ref[:, : width // 2] = front_ref[...]
    out_ref[:, width // 2 :] = back_ref[...]
    part = product(stacked(before), high_ref[0], low_ref[0], ROWS_ROWS)
    out_ref[:, :LEAF] += weight_of(weights_ref, 0, -1) * part
    part = product(stacked(after), high_ref[1], low_ref[1], ROWS_ROWS)
    out_ref[:, width - LEAF :] += weight_of(weights_ref, leaves - 1, 1) * part
    if not sums:
        return
    fields = dict(zip("rqdw", refs[:4]))
    locals_ = dict(zip("rqd", refs[4:7]))
    tile_ref = refs[-1]
    totals = {pair: jnp.zeros((rows, 1), jnp.float32) for pair in PAIRS}
    for leaf in range(leaves):
        here = {name: leaf_of(ref, leaf) for name, ref in fields.items()}
        here["z"] = leaf_of(out_ref, leaf)
        for left, right in PAIRS:
            terms = here[left] * here[right]
            if left + right == "rz":
                terms = terms + here["q"] * here["w"]
            totals[left + right] = totals[left + right] + row_sum(terms)
    for block in range(LOCAL):
        scale = 1.0 / (LEAF * (2 if block < 2 else 4))
        lanes = slice(block * LANES, (block + 1) * LANES)
        for name in "rqd":
            term = row_sum(locals_[name][:, lanes] * locals_["q"][:, lanes])
            totals[name + "z"] = totals[name + "z"] + scale * term
    tile_ref[...] = sums_tile([totals[pair] for pair in PAIRS], rows, PRODUCTS_TILE)


def first_combine_kernel(products, cluster, *refs):
    core_ref, mine_ref, other_ref, tile_ref = refs[:4]
    message_ref, level_ref = refs[-2:]
    own = level_ref.shape[0]
    depth = tile_ref.shape[0]
    total = mine_ref[...] + other_ref[...]
    level = total[:own]
    level_ref[...] = level
    tile = tile_ref[...]
    if products:
        partners = [refs[4][:own], level, refs[5][:own]]
        columns = [row_sum(level * partner) * (1.0 / cluster) for partner in partners]
        tile = tile + level_terms(core_ref[0], columns, 2 * own, depth)
    left = total.shape[0] - own
    message_ref[:left] = total[own:]
    message_ref[left:] = tile


def combine_kernel(products, last, sibling, own, bits, clusters, *refs):
    refs = list(refs)
    core_ref, mine_ref = refs[:2]
    got = [ref[...] for ref in refs[2 : 2 + 2 ** len(bits) - 1]]
    refs = refs[1 + 2 ** len(bits) :]
    sibling_ref = refs.pop() if sibling else None
    level_out = [] if last else [refs.pop() for _ in bits][::-1]
    next_ref = refs.pop()
    depth = PRODUCTS_TILE if products else NORM_TILE
    near = mine_ref[...] + got[0]
    total = near
    pairs = [(near[:own], bits[0], 0, clusters[0])]
    if len(bits) == 2:
        far = got[1] + got[2]
        total = near + far
        if sibling:
            sibling_ref[...] = far[:own]
        pairs.append((far[:own], None, 1, clusters[0]))
        pairs.append((total[own : 2 * own], bits[1], 0, clusters[1]))
    for ref, pair in zip(level_out, pairs[:: 2 if len(bits) == 2 else 1]):
        ref[...] = pair[0]
    tile = total[total.shape[0] - depth :]
    if products:
        r_ref, d_ref = refs[:2]
        refs = refs[2:]
        siblings = [refs.pop(0), refs.pop(0)] if len(bits) == 2 else []
        columns = [jnp.zeros((own, 1), jnp.float32)] * 3
        for level, bit, kind, cluster in pairs:
            if kind:
                partners = [siblings[0][...], level, siblings[1][...]]
            else:
                here = slice(bit * own, (bit + 1) * own)
                partners = [r_ref[here], level, d_ref[here]]
            terms = [row_sum(level * partner) * (1.0 / cluster) for partner in partners]
            columns = [column + term for column, term in zip(columns, terms)]
        tile = tile + level_terms(core_ref[0], columns, 2 * own, depth)
    left = total.shape[0] - depth - len(bits) * own
    if not last:
        next_ref[:left] = total[len(bits) * own : len(bits) * own + left]
        next_ref[left:] = tile
    else:
        for index, ref in enumerate(refs):
            next_ref[index * own : (index + 1) * own] = ref[...]
        for bit, pair in zip(bits, pairs[:: 2 if len(bits) == 2 else 1]):
            next_ref[bit * own : (bit + 1) * own] = pair[0]
        next_ref[next_ref.shape[0] - depth :] = tile


def up_parts(core, mine_ref, other_ref, local_ref, rows, width, depth):
    own = rows // 2
    crossing = (mine_ref.shape[0] - depth) // own
    sums = (mine_ref[crossing * own :] + other_ref[crossing * own :]).T[:rows]
    scaled = []
    for bit in range(crossing):
        here = slice(bit * own, (bit + 1) * own)
        low_rows = chosen(core, other_ref[here], mine_ref[here])
        high_rows = chosen(core, mine_ref[here], other_ref[here])
        scaled.append(jnp.concatenate([low_rows, high_rows], axis=0) * (1.0 / (width * (2 << bit))))
    one = [local_ref[:, part * LANES : (part + 1) * LANES] * (1.0 / (2 * LEAF)) for part in range(2)]
    two = local_ref[:, 2 * LANES :] * (1.0 / (4 * LEAF))
    return sums, [stacked(jnp.concatenate([one[part], two] + scaled, axis=1)) for part in range(2)]


def own_rows(core, column, crossing):
    own = column.shape[0] // 2
    return jnp.concatenate([chosen(core, column[own:], column[:own])] * crossing, axis=0)


def put_edges(core, field_ref, paired_ref, send_ref):
    rows = paired_ref.shape[0]
    paired_ref[...], send_ref[:rows] = sides(core, field_ref)
    send_ref[rows:] = jnp.zeros((SPARE, LEAF), jnp.float32)


def residual_up_kernel(first, siblings, *refs):
    core_ref, high_ref, low_ref, near_ref, mine_ref, other_ref, local_ref = refs[:7]
    refs = refs[7:]
    if first:
        image_ref, state_ref, paired_ref, send_ref = refs
        q_ref = image_ref
    else:
        field_ref, old_d_ref, old_q_ref, old_skel_ref, old_local_ref, old_state_ref = refs[:6]
        r_siblings = refs[6 : 6 + siblings]
        d_siblings = refs[6 + siblings : 6 + 2 * siblings]
        refs = refs[6 + 2 * siblings :]
        image_ref, state_ref, paired_ref, send_ref, d_ref, q_ref, skel_ref, new_local_ref = refs[:8]
        new_siblings = refs[8:]
    core = core_ref[0]
    rows, width = near_ref.shape
    half = width // 2
    sums, stacks = up_parts(core, mine_ref, other_ref, local_ref, rows, width, NORM_TILE)
    norm = sums[:, 0:1]
    state_ref[...] = in_lanes([norm], (rows, LANES))
    ratio = None if first else norm / old_state_ref[:, 0:1]
    for part in range(2):
        points = slice(part * half, (part + 1) * half)
        image = near_ref[:, points] + product(stacks[part], high_ref[:, points], low_ref[:, points], ROWS_COLS)
        image_ref[:, points] = image
        if not first:
            d_ref[:, points] = field_ref[:, points] + ratio * old_d_ref[:, points]
            q_ref[:, points] = image + ratio * old_q_ref[:, points]
    put_edges(core, q_ref, paired_ref, send_ref)
    if not first:
        rows_in = skel_ref.shape[0]
        crossing = rows_in // (rows // 2)
        skel_ref[...] = mine_ref[:rows_in] + own_rows(core, ratio, crossing) * old_skel_ref[...]
        new_local_ref[...] = local_ref[...] + ratio * old_local_ref[...]
        own_ratio = own_rows(core, ratio, 1)
        for new_ref, r_ref, d_ref in zip(new_siblings, r_siblings, d_siblings):
            new_ref[...] = r_ref[...] + own_ratio * d_ref[...]


def image_up_kernel(first, last, siblings, *refs):
    core_ref, high_ref, low_ref, near_ref, mine_ref, other_ref, local_ref = refs[:7]
    r_ref, w_ref, d_ref, q_ref, state_ref = refs[7:12]
    refs = refs[12:]
    if not first:
        solution_ref = refs[0]
        refs = refs[1:]
    if not last:
        r_skel_ref, d_skel_ref, r_local_ref, d_local_ref = refs[:4]
        r_siblings, q_siblings, d_siblings = [
            refs[4 + index * siblings : 4 + (index + 1) * siblings] for index in range(3)
        ]
        refs = refs[4 + 3 * siblings :]
    new_solution_ref, new_r_ref = refs[:2]
    if not last:
        new_d_ref, new_q_ref, new_skel_ref, new_local_ref, new_state_ref, paired_ref, send_ref = refs[2:9]
        new_siblings = refs[9:]
    core = core_ref[0]
    rows, width = near_ref.shape
    half = width // 2
    sums, stacks = up_parts(core, mine_ref, other_ref, local_ref, rows, width, PRODUCTS_TILE)
    dot = {pair: sums[:, index : index + 1] for index, pair in enumerate(PAIRS)}
    norm = state_ref[:, 0:1]
    step = norm / dot["dq"]
    new_norm = norm - step * (2.0 * dot["rq"] - step * dot["qq"])
    ratio = new_norm / norm
    curve = dot["rw"] - step * (dot["rz"] - step * dot["qz"])
    curve = curve + ratio * (dot["dw"] - step * dot["dz"] + dot["rq"] - step * dot["qq"] + ratio * dot["dq"])
    new_step = new_norm / curve
    for part in range(2):
        points = slice(part * half, (part + 1) * half)
        image = near_ref[:, points] + product(stacks[part], high_ref[:, points], low_ref[:, points], ROWS_COLS)
        d = d_ref[:, points]
        q = q_ref[:, points]
        r = r_ref[:, points] - step * q
        new_q = w_ref[:, points] - step * image + ratio * q
        new_d = r + ratio * d
        moved = step * d + new_step * new_d
        new_solution_ref[:, points] = moved if first else solution_ref[:, points] + moved
        new_r_ref[:, points] = r - new_step * new_q
        if not last:
            new_d_ref[:, points] = new_d
            new_q_ref[:, points] = new_q
    if not last:
        rows_in = new_skel_ref.shape[0]
        crossing = rows_in // (rows // 2)
        r_skel = r_skel_ref[:rows_in] - own_rows(core, step, crossing) * mine_ref[:rows_in]
        new_skel_ref[...] = r_skel + own_rows(core, ratio, crossing) * d_skel_ref[:rows_in]
        new_local_ref[...] = r_local_ref[...] - step * local_ref[...] + ratio * d_local_ref[...]
        own_step, own_ratio = own_rows(core, step, 1), own_rows(core, ratio, 1)
        for new_ref, r_ref, q_ref, d_ref in zip(new_siblings, r_siblings, q_siblings, d_siblings):
            new_ref[...] = r_ref[...] - own_step * q_ref[...] + own_ratio * d_ref[...]
        new_state_ref[...] = in_lanes([new_norm], (rows, LANES))
        put_edges(core, new_r_ref, paired_ref, send_ref)


def per_device(rhs, coords, nugget, near_ids, basis):
    rows, width = rhs.shape
    levels = basis.shape[0]
    leaves = width // LEAF
    own = rows // 2
    crossing = levels - (leaves.bit_length() - 1)
    devices = lax.axis_size("row") * lax.axis_size("col")
    place = jnp.reshape(lax.axis_index(BOTH), (1,))
    core = place % 2
    nugget = nugget[None, :]
    weights = leaf_weights(near_ids, place[0] * leaves)

    stages = [list(range(bit, min(bit + 2, crossing))) for bit in range(1, crossing, 2)]
    siblings = sum(len(bits) == 2 for bits in stages)

    def swap(value, mask):
        return lax.ppermute(value, BOTH, [(source, source ^ mask) for source in range(devices)])

    def halo(paired, other):
        outward = [(index, index + 1) for index in range(1, devices - 1, 2)]
        ends = [(0, 0), (devices - 1, devices - 1)]
        other = lax.ppermute(other, BOTH, outward + [(target, source) for source, target in outward] + ends)
        return swap(paired, 1), other

    def down(field, *tile):
        shapes = [f32(rows, LOCAL * LANES), f32(crossing * own, LANES)]
        shapes = shapes + [f32(crossing * own, LANES)] + list(tile)
        return call(down_kernel, shapes, core, field, high, low, scalars=1, flops=FLOPS if opening else 0, traffic=2**20 if opening else 0)

    def inner(half, field):
        args = [weights, field, nugget, *front_matrices, *back_matrices]
        body = functools.partial(inner_kernel, half)
        return call(body, [f32(rows, width // 2)], *args, flops=FLOPS // 2 if opening else 0)[0]

    def edge(paired, other, front, back, *more):
        shapes = [f32(rows, width)] + ([f32(PRODUCTS_TILE, LANES)] if more else [])
        args = [core, weights, paired, other, *outside, front, back, *more]
        return call(functools.partial(edge_kernel, bool(more)), shapes, *args, scalars=1, flops=FLOPS // 3 if opening else 0)

    def chain(products, final, keep, got, tile, beside_steps, r_skel=None, d_skel=None, r_sib=(), d_sib=()):
        depth = PRODUCTS_TILE if products else NORM_TILE
        results = []
        both = [r_skel, d_skel] if products else []
        message, level = call(
            functools.partial(first_combine_kernel, products, 2 * width),
            [f32((crossing - 1) * own + depth, LANES), f32(own, LANES)],
            core,
            keep,
            got,
            tile,
            *both,
            scalars=1,
        )
        done, kept = [level], []
        for index in range(len(stages) + 1):
            bits = stages[index] if index < len(stages) else []
            masks = [sum(1 << bit for at, bit in enumerate(bits) if pick >> at & 1) for pick in range(1, 2 ** len(bits))]
            got = [swap(message, mask) for mask in masks or [1]]
            if index < len(beside_steps):
                *got, result = lax.optimization_barrier((*got, beside_steps[index](message)))
                results.append(result)
            if not bits:
                break
            left = crossing - bits[-1] - 1
            paired = len(bits) == 2
            args = [core, message, *got, *both]
            if products and paired:
                args = args + [r_sib[index], d_sib[index]]
            sibling = paired and not final
            clusters = [width * (2 << bit) for bit in bits]
            message, *levels_out = call(
                functools.partial(combine_kernel, products, not left, sibling, own, bits, clusters),
                [f32((left or crossing) * own + depth, LANES)] + [f32(own, LANES)] * ((len(bits) if left else 0) + sibling),
                *args,
                *([] if left else done),
                scalars=1,
            )
            kept = kept + levels_out[len(levels_out) - sibling :]
            done = done + levels_out[: len(levels_out) - sibling]
        return message, got[0], results, kept

    groups = row_groups(leaves)
    turned = pltpu.VMEM((width, 8), jnp.float32)
    *front_matrices, high, low, lanes = pl.pallas_call(
        functools.partial(setup_kernel, groups[:1]),
        out_shape=[bf16(2, LEAF, LEAF)] * 2
        + [pltpu.VMEM((levels * LANES, width), jnp.bfloat16)] * 2
        + [f32(8, width)],
        in_specs=[whole(), whole(pltpu.HBM)],
        out_specs=[whole()] * 5,
        scratch_shapes=[turned, pltpu.VMEM(basis.shape, jnp.float32), pltpu.SemaphoreType.DMA((levels,))],
        compiler_params=pltpu.CompilerParams(vmem_limit_bytes=44 * 2**20),
        cost_estimate=pl.CostEstimate(flops=FLOPS, bytes_accessed=2**20, transcendentals=0),
    )(coords, basis)
    edges = call(edges_kernel, [f32(rows + 8, LEAF)] * 2, core, rhs, lanes, scalars=1)
    back_matrices = outside = None

    def after(message, *values):
        return lax.optimization_barrier((message, *values))[1:]

    def late_matrices(message):
        def body(lane_ref, high_ref, low_ref, sub_ref):
            fill_matrices(groups[1:], lane_ref, sub_ref, high_ref, low_ref)

        shapes = [bf16(2 * leaves - 3, LEAF, LEAF)] * 2
        return call(body, shapes, *after(message, lanes), flops=2 * FLOPS, scratch=[turned])

    def late_edge_matrices(message):
        def body(core_ref, *refs):
            edge_matrices(core_ref, rows, *refs)

        args = after(message, lanes, *edges)
        return call(body, [bf16(2, LEAF, LEAF)] * 2, core, *args, scalars=1, flops=FLOPS, scratch=[turned])

    solution, r, carried, opening = None, rhs, None, True
    for step in range(0, ITERS, 2):
        first, last = step == 0, step + 2 == ITERS
        r_local, keep, part, tile = down(r, f32(NORM_TILE, LANES))
        if first:
            edges = halo(*lax.optimization_barrier((part, *edges))[1:])
        got = swap(part, 1)
        if first:
            message, got, results, r_sib = chain(False, False, keep, got, tile, [late_matrices, late_edge_matrices])
            back_matrices, outside = results
            (near,) = edge(*edges, inner(0, r), inner(1, r))
        else:
            fronts = []

            def inner_work(message):
                fronts.extend(inner(half, *after(message, r)) for half in range(2))
                return fronts

            def edge_work(message):
                return edge(*edges, *after(message, *fronts))[0]

            message, got, results, r_sib = chain(False, False, keep, got, tile, [inner_work, edge_work])
            near = results[1]
        args = [core, high, low, near, message, got, r_local]
        outs = [f32(rows, width), f32(rows, LANES), f32(rows, LEAF), f32(rows + SPARE, LEAF)]
        if first:
            w, state, *edges = call(
                functools.partial(residual_up_kernel, True, 0), outs, *args, scalars=1, flops=FLOPS // 2
            )
            d, q, d_skel, d_local, d_sib = r, w, message, r_local, r_sib
        else:
            outs = outs + [f32(rows, width)] * 2 + [f32(crossing * own, LANES), f32(rows, LOCAL * LANES)]
            outs = outs + [f32(own, LANES)] * siblings
            body = functools.partial(residual_up_kernel, False, siblings)
            args = args + [r, *carried, *r_sib, *d_sib]
            w, state, paired, other, d, q, d_skel, d_local, *d_sib = call(
                body, outs, *args, scalars=1, flops=FLOPS // 2
            )
            edges = (paired, other)
        r_skel, opening = message, False
        edges = halo(*edges)
        q_local, keep, part = down(q)
        got = swap(part, 1)
        parts = [inner(half, q) for half in range(2)]
        near, tile = edge(*edges, *parts, r, q, d, w, r_local, q_local, d_local)
        message, got, _, q_sib = chain(True, last, keep, got, tile, [], r_skel, d_skel, r_sib, d_sib)
        args = [core, high, low, near, message, got, q_local, r, w, d, q, state]
        args = args + ([] if first else [solution]) + ([] if last else [r_skel, d_skel, r_local, d_local, *r_sib, *q_sib, *d_sib])
        outs = [f32(rows, width)] * 2
        if not last:
            outs = outs + [f32(rows, width)] * 2 + [f32(crossing * own, LANES), f32(rows, LOCAL * LANES)]
            outs = outs + [f32(rows, LANES), f32(rows, LEAF), f32(rows + SPARE, LEAF)] + [f32(own, LANES)] * siblings
        solution, r, *rest = call(
            functools.partial(image_up_kernel, first, last, siblings), outs, *args, scalars=1, flops=FLOPS // 2
        )
        if not last:
            carried = rest[:5]
            edges = halo(*rest[5:7])
            d_sib = rest[7:]
    return (solution, r)


def solution(mesh):
    placed = (
        P(None, BOTH),
        P(None, BOTH),
        P(BOTH),
        P(BOTH, None),
        P(None, None, BOTH),
    )
    return jax.shard_map(
        per_device,
        mesh=mesh,
        in_specs=placed,
        out_specs=(P(None, BOTH), P(None, BOTH)),
        check_vma=False,
    )
```

profile of v0, /device:TPU:0, one launch (start us, length us, event | category | flops | bytes accessed | tf_op | source)
XLA Modules:
  0.0 113.0 jit_solution(14271325914792002746)
XLA Ops:
  1.4 3.5 %shard_map.68 = (bf16[2,512,512]{2,1,0:T(8,128)(2,1)S(1)}, bf16[2,512,512]{2,1,0:T(8,128)(2,1)S(1)}, bf16[896,2048]{1,0:T(8,128)(2,1)S(1)}, bf16[896,2048]{1,0:T(8,128)(2,1)S(1)}, f32[8,2048]{1,0:T(8,128)S(1)}) custom-call(f32[3,2048]{1,0:T(4,128)S(1)} %copy-done.6, f32[7,128,2048]{2,1,0:T(8,128)} %basis_ref.1), custom_call_target="tpu_custom_call" | custom-call | flops 3000000000 | bytes 1048576 | tf_op jit(solution)/shard_map/pallas_call | solution.py:553
  4.9 2.3 %shard_map.69 = (f32[32,384]{1,0:T(8,128)S(1)}, f32[80,128]{1,0:T(8,128)S(1)}, f32[80,128]{1,0:T(8,128)S(1)}, f32[8,128]{1,0:T(8,128)S(1)}) custom-call(s32[1]{0:T(128)S(6)} %select_n.15.core_ref.refs_0_, f32[32,2048]{1,0:T(8,128)S(1)} %copy-done.4, bf16[896,2048]{1,0:T(8,128)(2,1)S(1)} %get-tuple-element.111.high_ref.refs_1_, ...), custom_call_target="tpu_custom_call" | custom-call | flops 3000000000 | bytes 1048576 | tf_op jit(solution)/shard_map/pallas_call | solution.py:83
  9.5 5.4 %collective-permute-start.5 = (f32[72,128]{1,0:T(8,128)S(1)}, f32[72,128]{1,0:T(8,128)S(1)}, u32[]{:S(2)}, u32[]{:S(2)}) collective-permute-start(f32[72,128]{1,0:T(8,128)S(1)} %get-tuple-element.121.refs_1_), channel_id=1, source_target_pairs={{0,6},{1,7},{2,4},{3,5},{4,2},{5,3},{6,0},{7,1},{8,14},{9,15},{10,... | collective-permute-start | bytes 110600 | tf_op jit(solution)/shard_map/ppermute | solution.py:486
  16.4 5.6 %shard_map.72 = (bf16[5,512,512]{2,1,0:T(8,128)(2,1)S(1)}, bf16[5,512,512]{2,1,0:T(8,128)(2,1)S(1)}) custom-call(f32[8,2048]{1,0:T(8,128)S(1)} %get-tuple-element.129.lane_ref.refs_0_), custom_call_target="tpu_custom_call" | custom-call | flops 6000000000 | bytes 1048576 | tf_op jit(solution)/shard_map/pallas_call | solution.py:83
  22.0 5.1 %collective-permute-start.8 = (f32[40,128]{1,0:T(8,128)S(1)}, f32[40,128]{1,0:T(8,128)S(1)}, u32[]{:S(2)}, u32[]{:S(2)}) collective-permute-start(f32[40,128]{1,0:T(8,128)S(1)} %get-tuple-element.128.refs_1_), channel_id=1, source_target_pairs={{0,24},{1,25},{2,26},{3,27},{4,28},{5,29},{6,30},{7,31},{8,16},{9,... | collective-permute-start | bytes 61448 | tf_op jit(solution)/shard_map/ppermute | solution.py:486
  30.2 3.0 %shard_map.74 = (bf16[2,512,512]{2,1,0:T(8,128)(2,1)S(1)}, bf16[2,512,512]{2,1,0:T(8,128)(2,1)S(1)}) custom-call(s32[1]{0:T(128)S(6)} %select_n.15.core_ref.refs_0_, f32[8,2048]{1,0:T(8,128)S(1)} %get-tuple-element.129.lane_ref.refs_0_, f32[40,512]{1,0:T(8,128)S(1)} %collective-permute-done.refs_1_.refs_2_, f32[40,512]{1,0:T(8,128)S(1)} %collective-permute-done.1.refs_2_.refs_3_), custom_call_target="tpu_custom_call" | custom-call | flops 3000000000 | bytes 1048576 | tf_op jit(solution)/shard_map/pallas_call | solution.py:83
  38.9 2.3 %shard_map.82 = (f32[32,384]{1,0:T(8,128)S(1)}, f32[80,128]{1,0:T(8,128)S(1)}, f32[80,128]{1,0:T(8,128)S(1)}) custom-call(s32[1]{0:T(128)S(6)} %select_n.15.core_ref.refs_0_, f32[32,2048]{1,0:T(8,128)S(1)} %get-tuple-element.150.field_ref.refs_9_.refs_11_.refs_8_.refs_10_, bf16[896,2048]{1,0:T(8,128)(2,1)S(1)} %copy-done.1, bf16[896,2048]{1,0:T(8,128)(2,1)S(1)} %copy-done.3), custom_call_target="tpu_custom_call" | custom-call | tf_op jit(solution)/shard_map/pallas_call | solution.py:83
  44.8 3.8 %collective-permute-start.15 = (f32[72,128]{1,0:T(8,128)S(1)}, f32[72,128]{1,0:T(8,128)S(1)}, u32[]{:S(2)}, u32[]{:S(2)}) collective-permute-start(f32[72,128]{1,0:T(8,128)S(1)} %get-tuple-element.156.refs_1_), channel_id=1, source_target_pairs={{0,6},{1,7},{2,4},{3,5},{4,2},{5,3},{6,0},{7,1},{8,14},{9,15},{10,... | collective-permute-start | bytes 110600 | tf_op jit(solution)/shard_map/ppermute | solution.py:486
  49.3 1.5 %collective-permute-done.15.refs_4_ = f32[72,128]{1,0:T(8,128)S(1)} collective-permute-done((f32[72,128]{1,0:T(8,128)S(1)}, f32[72,128]{1,0:T(8,128)S(1)}, u32[]{:S(2)}, u32[]{:S(2)}) %collective-permute-start.15) | collective-permute-done | bytes 36896 | tf_op jit(solution)/shard_map/ppermute | solution.py:486
  50.7 1.8 %collective-permute-done.14.refs_3_ = f32[72,128]{1,0:T(8,128)S(1)} collective-permute-done((f32[72,128]{1,0:T(8,128)S(1)}, f32[72,128]{1,0:T(8,128)S(1)}, u32[]{:S(2)}, u32[]{:S(2)}) %collective-permute-start.14) | collective-permute-done | bytes 36896 | tf_op jit(solution)/shard_map/ppermute | solution.py:486
  52.8 3.6 %collective-permute-start.18 = (f32[40,128]{1,0:T(8,128)S(1)}, f32[40,128]{1,0:T(8,128)S(1)}, u32[]{:S(2)}, u32[]{:S(2)}) collective-permute-start(f32[40,128]{1,0:T(8,128)S(1)} %get-tuple-element.158.refs_1_), channel_id=1, source_target_pairs={{0,24},{1,25},{2,26},{3,27},{4,28},{5,29},{6,30},{7,31},{8,16},{9,... | collective-permute-start | bytes 61448 | tf_op jit(solution)/shard_map/ppermute | solution.py:486
  58.5 2.6 %collective-permute-done.17.refs_3_ = f32[40,128]{1,0:T(8,128)S(1)} collective-permute-done((f32[40,128]{1,0:T(8,128)S(1)}, f32[40,128]{1,0:T(8,128)S(1)}, u32[]{:S(2)}, u32[]{:S(2)}) %collective-permute-start.17) | collective-permute-done | bytes 20512 | tf_op jit(solution)/shard_map/ppermute | solution.py:486
  64.0 2.3 %shard_map.88 = (f32[32,384]{1,0:T(8,128)S(1)}, f32[80,128]{1,0:T(8,128)S(1)}, f32[80,128]{1,0:T(8,128)S(1)}, f32[8,128]{1,0:T(8,128)S(1)}) custom-call(s32[1]{0:T(128)S(6)} %select_n.15.core_ref.refs_0_, f32[32,2048]{1,0:T(8,128)S(1)} %get-tuple-element.172.field_ref.refs_7_.refs_8_, bf16[896,2048]{1,0:T(8,128)(2,1)S(1)} %copy-done.1, ...), custom_call_target="tpu_custom_call" | custom-call | tf_op jit(solution)/shard_map/pallas_call | solution.py:83
  67.2 1.9 %collective-permute-start.27 = (f32[32,512]{1,0:T(8,128)S(1)}, f32[32,512]{1,0:T(8,128)S(1)}, u32[]{:S(2)}, u32[]{:S(2)}) collective-permute-start(f32[32,512]{1,0:T(8,128)S(1)} %get-tuple-element.177), channel_id=1, source_target_pairs={{0,1},{1,0},{2,3},{3,2},{4,5},{5,4},{6,7},{7,6},{8,9},{9,8},{10,11... | collective-permute-start | bytes 196616 | tf_op jit(solution)/shard_map/ppermute | solution.py:486
  69.1 1.9 %collective-permute-start.23 = (f32[72,128]{1,0:T(8,128)S(1)}, f32[72,128]{1,0:T(8,128)S(1)}, u32[]{:S(2)}, u32[]{:S(2)}) collective-permute-start(f32[72,128]{1,0:T(8,128)S(1)} %get-tuple-element.171.refs_1_), channel_id=1, source_target_pairs={{0,6},{1,7},{2,4},{3,5},{4,2},{5,3},{6,0},{7,1},{8,14},{9,15},{10,... | collective-permute-start | bytes 110600 | tf_op jit(solution)/shard_map/ppermute | solution.py:486
  76.2 2.9 %collective-permute-start.26 = (f32[40,128]{1,0:T(8,128)S(1)}, f32[40,128]{1,0:T(8,128)S(1)}, u32[]{:S(2)}, u32[]{:S(2)}) collective-permute-start(f32[40,128]{1,0:T(8,128)S(1)} %get-tuple-element.176.refs_1_), channel_id=1, source_target_pairs={{0,24},{1,25},{2,26},{3,27},{4,28},{5,29},{6,30},{7,31},{8,16},{9,... | collective-permute-start | bytes 61448 | tf_op jit(solution)/shard_map/ppermute | solution.py:486
  79.2 1.5 %collective-permute-start.24 = (f32[40,128]{1,0:T(8,128)S(1)}, f32[40,128]{1,0:T(8,128)S(1)}, u32[]{:S(2)}, u32[]{:S(2)}) collective-permute-start(f32[40,128]{1,0:T(8,128)S(1)} %get-tuple-element.176.refs_1_), channel_id=1, source_target_pairs={{0,8},{1,9},{2,10},{3,11},{4,12},{5,13},{6,14},{7,15},{8,0},{9,1},... | collective-permute-start | bytes 61448 | tf_op jit(solution)/shard_map/ppermute | solution.py:486
  81.8 1.9 %collective-permute-done.25.refs_3_ = f32[40,128]{1,0:T(8,128)S(1)} collective-permute-done((f32[40,128]{1,0:T(8,128)S(1)}, f32[40,128]{1,0:T(8,128)S(1)}, u32[]{:S(2)}, u32[]{:S(2)}) %collective-permute-start.25) | collective-permute-done | bytes 20512 | tf_op jit(solution)/shard_map/ppermute | solution.py:486
  87.4 1.9 %collective-permute-start.30 = (f32[32,512]{1,0:T(8,128)S(1)}, f32[32,512]{1,0:T(8,128)S(1)}, u32[]{:S(2)}, u32[]{:S(2)}) collective-permute-start(f32[32,512]{1,0:T(8,128)S(1)} %get-tuple-element.199), channel_id=1, source_target_pairs={{0,1},{1,0},{2,3},{3,2},{4,5},{5,4},{6,7},{7,6},{8,9},{9,8},{10,11... | collective-permute-start | bytes 196616 | tf_op jit(solution)/shard_map/ppermute | solution.py:486
  89.4 2.3 %shard_map.98 = (f32[32,384]{1,0:T(8,128)S(1)}, f32[80,128]{1,0:T(8,128)S(1)}, f32[80,128]{1,0:T(8,128)S(1)}) custom-call(s32[1]{0:T(128)S(6)} %select_n.15.core_ref.refs_0_, f32[32,2048]{1,0:T(8,128)S(1)} %get-tuple-element.201.field_ref.refs_9_.refs_10_, bf16[896,2048]{1,0:T(8,128)(2,1)S(1)} %copy-done.1, bf16[896,2048]{1,0:T(8,128)(2,1)S(1)} %copy-done.3), custom_call_target="tpu_custom_call" | custom-call | tf_op jit(solution)/shard_map/pallas_call | solution.py:83
  95.3 2.5 %collective-permute-start.35 = (f32[72,128]{1,0:T(8,128)S(1)}, f32[72,128]{1,0:T(8,128)S(1)}, u32[]{:S(2)}, u32[]{:S(2)}) collective-permute-start(f32[72,128]{1,0:T(8,128)S(1)} %get-tuple-element.211.refs_1_), channel_id=1, source_target_pairs={{0,6},{1,7},{2,4},{3,5},{4,2},{5,3},{6,0},{7,1},{8,14},{9,15},{10,... | collective-permute-start | bytes 110600 | tf_op jit(solution)/shard_map/ppermute | solution.py:486
  100.2 1.6 %collective-permute-done.34.refs_3_ = f32[72,128]{1,0:T(8,128)S(1)} collective-permute-done((f32[72,128]{1,0:T(8,128)S(1)}, f32[72,128]{1,0:T(8,128)S(1)}, u32[]{:S(2)}, u32[]{:S(2)}) %collective-permute-start.34) | collective-permute-done | bytes 36896 | tf_op jit(solution)/shard_map/ppermute | solution.py:486
  105.5 2.1 %collective-permute-start.36 = (f32[40,128]{1,0:T(8,128)S(1)}, f32[40,128]{1,0:T(8,128)S(1)}, u32[]{:S(2)}, u32[]{:S(2)}) collective-permute-start(f32[40,128]{1,0:T(8,128)S(1)} %get-tuple-element.213.refs_1_), channel_id=1, source_target_pairs={{0,8},{1,9},{2,10},{3,11},{4,12},{5,13},{6,14},{7,15},{8,0},{9,1},... | collective-permute-start | bytes 61448 | tf_op jit(solution)/shard_map/ppermute | solution.py:486
  110.8 2.2 %shard_map.103 = (f32[32,2048]{1,0:T(8,128)}, f32[32,2048]{1,0:T(8,128)}) custom-call(s32[1]{0:T(128)S(6)} %select_n.15.core_ref.refs_0_, bf16[896,2048]{1,0:T(8,128)(2,1)S(1)} %copy-done.1, bf16[896,2048]{1,0:T(8,128)(2,1)S(1)} %copy-done.3, f32[32,2048]{1,0:T(8,128)S(1)} %get-tuple-element.206.refs_3_, f32[88,128]{1,0:T(8,128)S(1)} %shard_map.102.refs_4_, ...), custom_call_target="tpu_custom_call" | custom-call | flops 1500000000 | bytes 1048576 | tf_op jit(solution)/shard_map/pallas_call | solution.py:83
  (115 shorter events, 46.5 us)
Async XLA Ops:
  8.3 21.9 %collective-permute-start = (f32[40,512]{1,0:T(8,128)S(1)}, f32[40,512]{1,0:T(8,128)S(1)}, u32[]{:S(2)}, u32[]{:S(2)}) collective-permute-start(f32[40,512]{1,0:T(8,128)S(1)} %get-tuple-element.117), channel_id=1, source_target_pairs={{0,1},{1,0},{2,3},{3,2},{4,5},{5,4},{6,7},{7,6},{8,9},{9,8},{10,11... | collective-permute-start | bytes 245768 | tf_op jit(solution)/shard_map/ppermute | solution.py:486
  8.4 21.8 %collective-permute-start.1 = (f32[40,512]{1,0:T(8,128)S(1)}, f32[40,512]{1,0:T(8,128)S(1)}, u32[]{:S(2)}, u32[]{:S(2)}) collective-permute-start(f32[40,512]{1,0:T(8,128)S(1)} %get-tuple-element.118), channel_id=1, source_target_pairs={{1,2},{3,4},{5,6},{7,8},{9,10},{11,12},{13,14},{15,16},{17,18},{19... | collective-permute-start | bytes 245768 | tf_op jit(solution)/shard_map/ppermute | solution.py:491
  9.5 12.4 %collective-permute-start.5 = (f32[72,128]{1,0:T(8,128)S(1)}, f32[72,128]{1,0:T(8,128)S(1)}, u32[]{:S(2)}, u32[]{:S(2)}) collective-permute-start(f32[72,128]{1,0:T(8,128)S(1)} %get-tuple-element.121.refs_1_), channel_id=1, source_target_pairs={{0,6},{1,7},{2,4},{3,5},{4,2},{5,3},{6,0},{7,1},{8,14},{9,15},{10,... | collective-permute-start | bytes 110600 | tf_op jit(solution)/shard_map/ppermute | solution.py:486
  14.9 7.0 %collective-permute-start.4 = (f32[72,128]{1,0:T(8,128)S(1)}, f32[72,128]{1,0:T(8,128)S(1)}, u32[]{:S(2)}, u32[]{:S(2)}) collective-permute-start(f32[72,128]{1,0:T(8,128)S(1)} %get-tuple-element.121.refs_1_), channel_id=1, source_target_pairs={{0,4},{1,5},{2,6},{3,7},{4,0},{5,1},{6,2},{7,3},{8,12},{9,13},{10,... | collective-permute-start | bytes 110600 | tf_op jit(solution)/shard_map/ppermute | solution.py:486
  15.3 6.7 %collective-permute-start.3 = (f32[72,128]{1,0:T(8,128)S(1)}, f32[72,128]{1,0:T(8,128)S(1)}, u32[]{:S(2)}, u32[]{:S(2)}) collective-permute-start(f32[72,128]{1,0:T(8,128)S(1)} %get-tuple-element.121.refs_1_), channel_id=1, source_target_pairs={{0,2},{1,3},{2,0},{3,1},{4,6},{5,7},{6,4},{7,5},{8,10},{9,11},{10,... | collective-permute-start | bytes 110600 | tf_op jit(solution)/shard_map/ppermute | solution.py:486
  22.0 11.2 %collective-permute-start.8 = (f32[40,128]{1,0:T(8,128)S(1)}, f32[40,128]{1,0:T(8,128)S(1)}, u32[]{:S(2)}, u32[]{:S(2)}) collective-permute-start(f32[40,128]{1,0:T(8,128)S(1)} %get-tuple-element.128.refs_1_), channel_id=1, source_target_pairs={{0,24},{1,25},{2,26},{3,27},{4,28},{5,29},{6,30},{7,31},{8,16},{9,... | collective-permute-start | bytes 61448 | tf_op jit(solution)/shard_map/ppermute | solution.py:486
  27.1 6.1 %collective-permute-start.7 = (f32[40,128]{1,0:T(8,128)S(1)}, f32[40,128]{1,0:T(8,128)S(1)}, u32[]{:S(2)}, u32[]{:S(2)}) collective-permute-start(f32[40,128]{1,0:T(8,128)S(1)} %get-tuple-element.128.refs_1_), channel_id=1, source_target_pairs={{0,16},{1,17},{2,18},{3,19},{4,20},{5,21},{6,22},{7,23},{8,24},{9,... | collective-permute-start | bytes 61448 | tf_op jit(solution)/shard_map/ppermute | solution.py:486
  27.1 6.2 %collective-permute-start.6 = (f32[40,128]{1,0:T(8,128)S(1)}, f32[40,128]{1,0:T(8,128)S(1)}, u32[]{:S(2)}, u32[]{:S(2)}) collective-permute-start(f32[40,128]{1,0:T(8,128)S(1)} %get-tuple-element.128.refs_1_), channel_id=1, source_target_pairs={{0,8},{1,9},{2,10},{3,11},{4,12},{5,13},{6,14},{7,15},{8,0},{9,1},... | collective-permute-start | bytes 61448 | tf_op jit(solution)/shard_map/ppermute | solution.py:486
  36.6 7.1 %collective-permute-start.11 = (f32[40,512]{1,0:T(8,128)S(1)}, f32[40,512]{1,0:T(8,128)S(1)}, u32[]{:S(2)}, u32[]{:S(2)}) collective-permute-start(f32[40,512]{1,0:T(8,128)S(1)} %get-tuple-element.149), channel_id=1, source_target_pairs={{1,2},{3,4},{5,6},{7,8},{9,10},{11,12},{13,14},{15,16},{17,18},{19... | collective-permute-start | bytes 245768 | tf_op jit(solution)/shard_map/ppermute | solution.py:491
  37.5 6.2 %collective-permute-start.10 = (f32[32,512]{1,0:T(8,128)S(1)}, f32[32,512]{1,0:T(8,128)S(1)}, u32[]{:S(2)}, u32[]{:S(2)}) collective-permute-start(f32[32,512]{1,0:T(8,128)S(1)} %get-tuple-element.148), channel_id=1, source_target_pairs={{0,1},{1,0},{2,3},{3,2},{4,5},{5,4},{6,7},{7,6},{8,9},{9,8},{10,11... | collective-permute-start | bytes 196616 | tf_op jit(solution)/shard_map/ppermute | solution.py:486
  44.8 5.9 %collective-permute-start.15 = (f32[72,128]{1,0:T(8,128)S(1)}, f32[72,128]{1,0:T(8,128)S(1)}, u32[]{:S(2)}, u32[]{:S(2)}) collective-permute-start(f32[72,128]{1,0:T(8,128)S(1)} %get-tuple-element.156.refs_1_), channel_id=1, source_target_pairs={{0,6},{1,7},{2,4},{3,5},{4,2},{5,3},{6,0},{7,1},{8,14},{9,15},{10,... | collective-permute-start | bytes 110600 | tf_op jit(solution)/shard_map/ppermute | solution.py:486
  52.8 5.6 %collective-permute-start.18 = (f32[40,128]{1,0:T(8,128)S(1)}, f32[40,128]{1,0:T(8,128)S(1)}, u32[]{:S(2)}, u32[]{:S(2)}) collective-permute-start(f32[40,128]{1,0:T(8,128)S(1)} %get-tuple-element.158.refs_1_), channel_id=1, source_target_pairs={{0,24},{1,25},{2,26},{3,27},{4,28},{5,29},{6,30},{7,31},{8,16},{9,... | collective-permute-start | bytes 61448 | tf_op jit(solution)/shard_map/ppermute | solution.py:486
  56.4 4.7 %collective-permute-start.17 = (f32[40,128]{1,0:T(8,128)S(1)}, f32[40,128]{1,0:T(8,128)S(1)}, u32[]{:S(2)}, u32[]{:S(2)}) collective-permute-start(f32[40,128]{1,0:T(8,128)S(1)} %get-tuple-element.158.refs_1_), channel_id=1, source_target_pairs={{0,16},{1,17},{2,18},{3,19},{4,20},{5,21},{6,22},{7,23},{8,24},{9,... | collective-permute-start | bytes 61448 | tf_op jit(solution)/shard_map/ppermute | solution.py:486
  56.4 4.7 %collective-permute-start.16 = (f32[40,128]{1,0:T(8,128)S(1)}, f32[40,128]{1,0:T(8,128)S(1)}, u32[]{:S(2)}, u32[]{:S(2)}) collective-permute-start(f32[40,128]{1,0:T(8,128)S(1)} %get-tuple-element.158.refs_1_), channel_id=1, source_target_pairs={{0,8},{1,9},{2,10},{3,11},{4,12},{5,13},{6,14},{7,15},{8,0},{9,1},... | collective-permute-start | bytes 61448 | tf_op jit(solution)/shard_map/ppermute | solution.py:486
  66.6 14.1 %collective-permute-start.28 = (f32[40,512]{1,0:T(8,128)S(1)}, f32[40,512]{1,0:T(8,128)S(1)}, u32[]{:S(2)}, u32[]{:S(2)}) collective-permute-start(f32[40,512]{1,0:T(8,128)S(1)} %get-tuple-element.178), channel_id=1, source_target_pairs={{1,2},{3,4},{5,6},{7,8},{9,10},{11,12},{13,14},{15,16},{17,18},{19... | collective-permute-start | bytes 245768 | tf_op jit(solution)/shard_map/ppermute | solution.py:491
  67.2 13.4 %collective-permute-start.27 = (f32[32,512]{1,0:T(8,128)S(1)}, f32[32,512]{1,0:T(8,128)S(1)}, u32[]{:S(2)}, u32[]{:S(2)}) collective-permute-start(f32[32,512]{1,0:T(8,128)S(1)} %get-tuple-element.177), channel_id=1, source_target_pairs={{0,1},{1,0},{2,3},{3,2},{4,5},{5,4},{6,7},{7,6},{8,9},{9,8},{10,11... | collective-permute-start | bytes 196616 | tf_op jit(solution)/shard_map/ppermute | solution.py:486
  69.1 6.0 %collective-permute-start.23 = (f32[72,128]{1,0:T(8,128)S(1)}, f32[72,128]{1,0:T(8,128)S(1)}, u32[]{:S(2)}, u32[]{:S(2)}) collective-permute-start(f32[72,128]{1,0:T(8,128)S(1)} %get-tuple-element.171.refs_1_), channel_id=1, source_target_pairs={{0,6},{1,7},{2,4},{3,5},{4,2},{5,3},{6,0},{7,1},{8,14},{9,15},{10,... | collective-permute-start | bytes 110600 | tf_op jit(solution)/shard_map/ppermute | solution.py:486
  76.2 5.6 %collective-permute-start.26 = (f32[40,128]{1,0:T(8,128)S(1)}, f32[40,128]{1,0:T(8,128)S(1)}, u32[]{:S(2)}, u32[]{:S(2)}) collective-permute-start(f32[40,128]{1,0:T(8,128)S(1)} %get-tuple-element.176.refs_1_), channel_id=1, source_target_pairs={{0,24},{1,25},{2,26},{3,27},{4,28},{5,29},{6,30},{7,31},{8,16},{9,... | collective-permute-start | bytes 61448 | tf_op jit(solution)/shard_map/ppermute | solution.py:486
  79.1 4.7 %collective-permute-start.25 = (f32[40,128]{1,0:T(8,128)S(1)}, f32[40,128]{1,0:T(8,128)S(1)}, u32[]{:S(2)}, u32[]{:S(2)}) collective-permute-start(f32[40,128]{1,0:T(8,128)S(1)} %get-tuple-element.176.refs_1_), channel_id=1, source_target_pairs={{0,16},{1,17},{2,18},{3,19},{4,20},{5,21},{6,22},{7,23},{8,24},{9,... | collective-permute-start | bytes 61448 | tf_op jit(solution)/shard_map/ppermute | solution.py:486
  86.5 7.6 %collective-permute-start.31 = (f32[40,512]{1,0:T(8,128)S(1)}, f32[40,512]{1,0:T(8,128)S(1)}, u32[]{:S(2)}, u32[]{:S(2)}) collective-permute-start(f32[40,512]{1,0:T(8,128)S(1)} %get-tuple-element.200), channel_id=1, source_target_pairs={{1,2},{3,4},{5,6},{7,8},{9,10},{11,12},{13,14},{15,16},{17,18},{19... | collective-permute-start | bytes 245768 | tf_op jit(solution)/shard_map/ppermute | solution.py:491
  87.4 6.7 %collective-permute-start.30 = (f32[32,512]{1,0:T(8,128)S(1)}, f32[32,512]{1,0:T(8,128)S(1)}, u32[]{:S(2)}, u32[]{:S(2)}) collective-permute-start(f32[32,512]{1,0:T(8,128)S(1)} %get-tuple-element.199), channel_id=1, source_target_pairs={{0,1},{1,0},{2,3},{3,2},{4,5},{5,4},{6,7},{7,6},{8,9},{9,8},{10,11... | collective-permute-start | bytes 196616 | tf_op jit(solution)/shard_map/ppermute | solution.py:486
  95.3 4.9 %collective-permute-start.35 = (f32[72,128]{1,0:T(8,128)S(1)}, f32[72,128]{1,0:T(8,128)S(1)}, u32[]{:S(2)}, u32[]{:S(2)}) collective-permute-start(f32[72,128]{1,0:T(8,128)S(1)} %get-tuple-element.211.refs_1_), channel_id=1, source_target_pairs={{0,6},{1,7},{2,4},{3,5},{4,2},{5,3},{6,0},{7,1},{8,14},{9,15},{10,... | collective-permute-start | bytes 110600 | tf_op jit(solution)/shard_map/ppermute | solution.py:486
  103.2 5.6 %collective-permute-start.38 = (f32[40,128]{1,0:T(8,128)S(1)}, f32[40,128]{1,0:T(8,128)S(1)}, u32[]{:S(2)}, u32[]{:S(2)}) collective-permute-start(f32[40,128]{1,0:T(8,128)S(1)} %get-tuple-element.213.refs_1_), channel_id=1, source_target_pairs={{0,24},{1,25},{2,26},{3,27},{4,28},{5,29},{6,30},{7,31},{8,16},{9,... | collective-permute-start | bytes 61448 | tf_op jit(solution)/shard_map/ppermute | solution.py:486
  104.3 4.7 %collective-permute-start.37 = (f32[40,128]{1,0:T(8,128)S(1)}, f32[40,128]{1,0:T(8,128)S(1)}, u32[]{:S(2)}, u32[]{:S(2)}) collective-permute-start(f32[40,128]{1,0:T(8,128)S(1)} %get-tuple-element.213.refs_1_), channel_id=1, source_target_pairs={{0,16},{1,17},{2,18},{3,19},{4,20},{5,21},{6,22},{7,23},{8,24},{9,... | collective-permute-start | bytes 61448 | tf_op jit(solution)/shard_map/ppermute | solution.py:486
  (24 other events, 87.0 us)
where the time goes:
time: 113 us
  starting transfers between devices  46.7 us (41%)
  Pallas kernels  42.1 us (37%)
  waiting for transfers between devices  20.6 us (18%)
  local copies, waits for them, and re-layouts  2.26 us (2%)
    ppermute x36, starting transfers between devices, swap(): lax.ppermute(value, BOTH, [(source, source ^ mask) for source in range(de...  43.6 us
    pallas_call x35, Pallas kernels, call(): pl.pallas_call(body, out_shape=outs, in_specs=[whole(pltpu.SMEM)] * scala...  38.6 us
    ppermute x36, waiting for transfers between devices, swap(): lax.ppermute(value, BOTH, [(source, source ^ mask) for source in range(de...  20.6 us
    pallas_call x1, Pallas kernels, per_device(): pl.pallas_call(functools.partial(setup_kernel, groups[:1]), out_shape=[bf...  3.48 us
    ppermute x4, starting transfers between devices, halo(): lax.ppermute(other, BOTH, outward + [(target, source) for source, target...  3.04 us
  transfers between devices with their start and end apart: 40, of which 17 were waited for; matrix products, arithmetic and copies ran while one was open for 0% of the time, Pallas kernels for 23%

commit v1 on v0

--- a/solution.py
+++ b/solution.py
@@ -145,16 +145,16 @@
 def edge_matrices(core_ref, rows, lane_ref, paired_ref, other_ref, high_ref, low_ref, sub_ref):
     core = core_ref[0]
     leaves = lane_ref.shape[1] // LEAF
-    sub_ref[...] = lane_ref[...].T
     paired = paired_ref[rows : rows + 3]
     other = other_ref[rows : rows + 3]
     lanes = [chosen(core, paired, other), chosen(core, other, paired)]
 
     for side in range(2):
-        first_row = side * (leaves - 1) * LEAF
+        first_point = side * (leaves - 1) * LEAF
+        sub_ref[side * LEAF : (side + 1) * LEAF] = lane_ref[:, first_point : first_point + LEAF].T
 
         def one(part, carry):
-            row_at = pl.multiple_of(first_row + part * CHUNK, CHUNK)
+            row_at = pl.multiple_of(side * LEAF + part * CHUNK, CHUNK)
             out_at = pl.ds(pl.multiple_of(part * CHUNK, CHUNK), CHUNK)
             values = matrix_rows(sub_ref[pl.ds(row_at, CHUNK)], lanes[side])
             high_ref[side, out_at], low_ref[side, out_at] = values
@@ -485,11 +485,13 @@
     def swap(value, mask):
         return lax.ppermute(value, BOTH, [(source, source ^ mask) for source in range(devices)])
 
-    def halo(paired, other):
+    def far_halo(other):
         outward = [(index, index + 1) for index in range(1, devices - 1, 2)]
         ends = [(0, 0), (devices - 1, devices - 1)]
-        other = lax.ppermute(other, BOTH, outward + [(target, source) for source, target in outward] + ends)
-        return swap(paired, 1), other
+        return lax.ppermute(other, BOTH, outward + [(target, source) for source, target in outward] + ends)
+
+    def halo(paired, other):
+        return swap(paired, 1), far_halo(other)
 
     def down(field, *tile):
         shapes = [f32(rows, LOCAL * LANES), f32(crossing * own, LANES)]
@@ -553,7 +555,7 @@
     *front_matrices, high, low, lanes = pl.pallas_call(
         functools.partial(setup_kernel, groups[:1]),
         out_shape=[bf16(2, LEAF, LEAF)] * 2
-        + [pltpu.VMEM((levels * LANES, width), jnp.bfloat16)] * 2
+        + [bf16(levels * LANES, width)] * 2
         + [f32(8, width)],
         in_specs=[whole(), whole(pltpu.HBM)],
         out_specs=[whole()] * 5,
@@ -568,6 +570,8 @@
         return lax.optimization_barrier((message, *values))[1:]
 
     def late_matrices(message):
+        edges[0] = swap(after(message, edges[0])[0], 1)
+
         def body(lane_ref, high_ref, low_ref, sub_ref):
             fill_matrices(groups[1:], lane_ref, sub_ref, high_ref, low_ref)
 
@@ -579,14 +583,14 @@
             edge_matrices(core_ref, rows, *refs)
 
         args = after(message, lanes, *edges)
-        return call(body, [bf16(2, LEAF, LEAF)] * 2, core, *args, scalars=1, flops=FLOPS, scratch=[turned])
+        return call(body, [bf16(2, LEAF, LEAF)] * 2, core, *args, scalars=1, flops=FLOPS, scratch=[pltpu.VMEM((2 * LEAF, 8), jnp.float32)])
 
     solution, r, carried, opening = None, rhs, None, True
     for step in range(0, ITERS, 2):
         first, last = step == 0, step + 2 == ITERS
         r_local, keep, part, tile = down(r, f32(NORM_TILE, LANES))
         if first:
-            edges = halo(*lax.optimization_barrier((part, *edges))[1:])
+            edges = [edges[0], far_halo(lax.optimization_barrier((part, edges[1]))[1])]
         got = swap(part, 1)
         if first:
             message, got, results, r_sib = chain(False, False, keep, got, tile, [late_matrices, late_edge_matrices])

time: 113 us -> 113 us (level)
  no operation moved by 1% of the time
where the time goes in v1:
time: 113 us
  starting transfers between devices  46.6 us (41%)
  Pallas kernels  42 us (37%)
  waiting for transfers between devices  20.6 us (18%)
  local copies, waits for them, and re-layouts  2.26 us (2%)
    ppermute x36, starting transfers between devices, swap(): lax.ppermute(value, BOTH, [(source, source ^ mask) for source in range(de...  43.6 us
    pallas_call x35, Pallas kernels, call(): pl.pallas_call(body, out_shape=outs, in_specs=[whole(pltpu.SMEM)] * scala...  38.6 us
    ppermute x36, waiting for transfers between devices, swap(): lax.ppermute(value, BOTH, [(source, source ^ mask) for source in range(de...  20.6 us
    pallas_call x1, Pallas kernels, per_device(): pl.pallas_call(functools.partial(setup_kernel, groups[:1]), out_shape=[bf...  3.48 us
    ppermute x4, starting transfers between devices, far_halo(): lax.ppermute(other, BOTH, outward + [(target, source) for source, target...  3.05 us
  transfers between devices with their start and end apart: 40, of which 17 were waited for; matrix products, arithmetic and copies ran while one was open for 0% of the time, Pallas kernels for 23%

profile of v1, /device:TPU:0, one launch (start us, length us, event | category | flops | bytes accessed | tf_op | source)
XLA Modules:
  0.0 112.8 jit_solution(6698284171596637459)
XLA Ops:
  1.4 3.5 %shard_map.68 = (bf16[2,512,512]{2,1,0:T(8,128)(2,1)S(1)}, bf16[2,512,512]{2,1,0:T(8,128)(2,1)S(1)}, bf16[896,2048]{1,0:T(8,128)(2,1)S(1)}, bf16[896,2048]{1,0:T(8,128)(2,1)S(1)}, f32[8,2048]{1,0:T(8,128)S(1)}) custom-call(f32[3,2048]{1,0:T(4,128)S(1)} %copy-done.6, f32[7,128,2048]{2,1,0:T(8,128)} %basis_ref.1), custom_call_target="tpu_custom_call" | custom-call | flops 3000000000 | bytes 1048576 | tf_op jit(solution)/shard_map/pallas_call | solution.py:555
  4.9 2.3 %shard_map.69 = (f32[32,384]{1,0:T(8,128)S(1)}, f32[80,128]{1,0:T(8,128)S(1)}, f32[80,128]{1,0:T(8,128)S(1)}, f32[8,128]{1,0:T(8,128)S(1)}) custom-call(s32[1]{0:T(128)S(6)} %select_n.15.core_ref.refs_0_, f32[32,2048]{1,0:T(8,128)S(1)} %copy-done.4, bf16[896,2048]{1,0:T(8,128)(2,1)S(1)} %get-tuple-element.111.high_ref.refs_1_, ...), custom_call_target="tpu_custom_call" | custom-call | flops 3000000000 | bytes 1048576 | tf_op jit(solution)/shard_map/pallas_call | solution.py:83
  9.4 5.4 %collective-permute-start.5 = (f32[72,128]{1,0:T(8,128)S(1)}, f32[72,128]{1,0:T(8,128)S(1)}, u32[]{:S(2)}, u32[]{:S(2)}) collective-permute-start(f32[72,128]{1,0:T(8,128)S(1)} %get-tuple-element.116.refs_1_), channel_id=1, source_target_pairs={{0,6},{1,7},{2,4},{3,5},{4,2},{5,3},{6,0},{7,1},{8,14},{9,15},{10,... | collective-permute-start | bytes 110600 | tf_op jit(solution)/shard_map/ppermute | solution.py:486
  16.3 5.6 %shard_map.72 = (bf16[5,512,512]{2,1,0:T(8,128)(2,1)S(1)}, bf16[5,512,512]{2,1,0:T(8,128)(2,1)S(1)}) custom-call(f32[8,2048]{1,0:T(8,128)S(1)} %get-tuple-element.129.lane_ref.refs_0_), custom_call_target="tpu_custom_call" | custom-call | flops 6000000000 | bytes 1048576 | tf_op jit(solution)/shard_map/pallas_call | solution.py:83
  21.9 5.1 %collective-permute-start.8 = (f32[40,128]{1,0:T(8,128)S(1)}, f32[40,128]{1,0:T(8,128)S(1)}, u32[]{:S(2)}, u32[]{:S(2)}) collective-permute-start(f32[40,128]{1,0:T(8,128)S(1)} %get-tuple-element.128.refs_1_), channel_id=1, source_target_pairs={{0,24},{1,25},{2,26},{3,27},{4,28},{5,29},{6,30},{7,31},{8,16},{9,... | collective-permute-start | bytes 61448 | tf_op jit(solution)/shard_map/ppermute | solution.py:486
  30.1 2.9 %shard_map.74 = (bf16[2,512,512]{2,1,0:T(8,128)(2,1)S(1)}, bf16[2,512,512]{2,1,0:T(8,128)(2,1)S(1)}) custom-call(s32[1]{0:T(128)S(6)} %select_n.15.core_ref.refs_0_, f32[8,2048]{1,0:T(8,128)S(1)} %get-tuple-element.129.lane_ref.refs_0_, f32[40,512]{1,0:T(8,128)S(1)} %collective-permute-done.1.refs_1_.refs_2_, ...), custom_call_target="tpu_custom_call" | custom-call | flops 3000000000 | bytes 1048576 | tf_op jit(solution)/shard_map/pallas_call | solution.py:83
  38.8 2.3 %shard_map.82 = (f32[32,384]{1,0:T(8,128)S(1)}, f32[80,128]{1,0:T(8,128)S(1)}, f32[80,128]{1,0:T(8,128)S(1)}) custom-call(s32[1]{0:T(128)S(6)} %select_n.15.core_ref.refs_0_, f32[32,2048]{1,0:T(8,128)S(1)} %get-tuple-element.150.field_ref.refs_9_.refs_11_.refs_8_.refs_10_, bf16[896,2048]{1,0:T(8,128)(2,1)S(1)} %copy-done.1, bf16[896,2048]{1,0:T(8,128)(2,1)S(1)} %copy-done.3), custom_call_target="tpu_custom_call" | custom-call | tf_op jit(solution)/shard_map/pallas_call | solution.py:83
  44.7 3.8 %collective-permute-start.15 = (f32[72,128]{1,0:T(8,128)S(1)}, f32[72,128]{1,0:T(8,128)S(1)}, u32[]{:S(2)}, u32[]{:S(2)}) collective-permute-start(f32[72,128]{1,0:T(8,128)S(1)} %get-tuple-element.156.refs_1_), channel_id=1, source_target_pairs={{0,6},{1,7},{2,4},{3,5},{4,2},{5,3},{6,0},{7,1},{8,14},{9,15},{10,... | collective-permute-start | bytes 110600 | tf_op jit(solution)/shard_map/ppermute | solution.py:486
  49.1 1.5 %collective-permute-done.15.refs_4_ = f32[72,128]{1,0:T(8,128)S(1)} collective-permute-done((f32[72,128]{1,0:T(8,128)S(1)}, f32[72,128]{1,0:T(8,128)S(1)}, u32[]{:S(2)}, u32[]{:S(2)}) %collective-permute-start.15) | collective-permute-done | bytes 36896 | tf_op jit(solution)/shard_map/ppermute | solution.py:486
  50.6 1.8 %collective-permute-done.14.refs_3_ = f32[72,128]{1,0:T(8,128)S(1)} collective-permute-done((f32[72,128]{1,0:T(8,128)S(1)}, f32[72,128]{1,0:T(8,128)S(1)}, u32[]{:S(2)}, u32[]{:S(2)}) %collective-permute-start.14) | collective-permute-done | bytes 36896 | tf_op jit(solution)/shard_map/ppermute | solution.py:486
  52.7 3.6 %collective-permute-start.18 = (f32[40,128]{1,0:T(8,128)S(1)}, f32[40,128]{1,0:T(8,128)S(1)}, u32[]{:S(2)}, u32[]{:S(2)}) collective-permute-start(f32[40,128]{1,0:T(8,128)S(1)} %get-tuple-element.158.refs_1_), channel_id=1, source_target_pairs={{0,24},{1,25},{2,26},{3,27},{4,28},{5,29},{6,30},{7,31},{8,16},{9,... | collective-permute-start | bytes 61448 | tf_op jit(solution)/shard_map/ppermute | solution.py:486
  58.3 2.6 %collective-permute-done.17.refs_3_ = f32[40,128]{1,0:T(8,128)S(1)} collective-permute-done((f32[40,128]{1,0:T(8,128)S(1)}, f32[40,128]{1,0:T(8,128)S(1)}, u32[]{:S(2)}, u32[]{:S(2)}) %collective-permute-start.17) | collective-permute-done | bytes 20512 | tf_op jit(solution)/shard_map/ppermute | solution.py:486
  63.9 2.3 %shard_map.88 = (f32[32,384]{1,0:T(8,128)S(1)}, f32[80,128]{1,0:T(8,128)S(1)}, f32[80,128]{1,0:T(8,128)S(1)}, f32[8,128]{1,0:T(8,128)S(1)}) custom-call(s32[1]{0:T(128)S(6)} %select_n.15.core_ref.refs_0_, f32[32,2048]{1,0:T(8,128)S(1)} %get-tuple-element.172.field_ref.refs_7_.refs_8_, bf16[896,2048]{1,0:T(8,128)(2,1)S(1)} %copy-done.1, ...), custom_call_target="tpu_custom_call" | custom-call | tf_op jit(solution)/shard_map/pallas_call | solution.py:83
  67.1 1.9 %collective-permute-start.27 = (f32[32,512]{1,0:T(8,128)S(1)}, f32[32,512]{1,0:T(8,128)S(1)}, u32[]{:S(2)}, u32[]{:S(2)}) collective-permute-start(f32[32,512]{1,0:T(8,128)S(1)} %get-tuple-element.177), channel_id=1, source_target_pairs={{0,1},{1,0},{2,3},{3,2},{4,5},{5,4},{6,7},{7,6},{8,9},{9,8},{10,11... | collective-permute-start | bytes 196616 | tf_op jit(solution)/shard_map/ppermute | solution.py:486
  68.9 1.9 %collective-permute-start.23 = (f32[72,128]{1,0:T(8,128)S(1)}, f32[72,128]{1,0:T(8,128)S(1)}, u32[]{:S(2)}, u32[]{:S(2)}) collective-permute-start(f32[72,128]{1,0:T(8,128)S(1)} %get-tuple-element.171.refs_1_), channel_id=1, source_target_pairs={{0,6},{1,7},{2,4},{3,5},{4,2},{5,3},{6,0},{7,1},{8,14},{9,15},{10,... | collective-permute-start | bytes 110600 | tf_op jit(solution)/shard_map/ppermute | solution.py:486
  76.0 2.9 %collective-permute-start.26 = (f32[40,128]{1,0:T(8,128)S(1)}, f32[40,128]{1,0:T(8,128)S(1)}, u32[]{:S(2)}, u32[]{:S(2)}) collective-permute-start(f32[40,128]{1,0:T(8,128)S(1)} %get-tuple-element.176.refs_1_), channel_id=1, source_target_pairs={{0,24},{1,25},{2,26},{3,27},{4,28},{5,29},{6,30},{7,31},{8,16},{9,... | collective-permute-start | bytes 61448 | tf_op jit(solution)/shard_map/ppermute | solution.py:486
  79.0 1.5 %collective-permute-start.24 = (f32[40,128]{1,0:T(8,128)S(1)}, f32[40,128]{1,0:T(8,128)S(1)}, u32[]{:S(2)}, u32[]{:S(2)}) collective-permute-start(f32[40,128]{1,0:T(8,128)S(1)} %get-tuple-element.176.refs_1_), channel_id=1, source_target_pairs={{0,8},{1,9},{2,10},{3,11},{4,12},{5,13},{6,14},{7,15},{8,0},{9,1},... | collective-permute-start | bytes 61448 | tf_op jit(solution)/shard_map/ppermute | solution.py:486
  81.7 1.9 %collective-permute-done.25.refs_3_ = f32[40,128]{1,0:T(8,128)S(1)} collective-permute-done((f32[40,128]{1,0:T(8,128)S(1)}, f32[40,128]{1,0:T(8,128)S(1)}, u32[]{:S(2)}, u32[]{:S(2)}) %collective-permute-start.25) | collective-permute-done | bytes 20512 | tf_op jit(solution)/shard_map/ppermute | solution.py:486
  87.3 1.9 %collective-permute-start.30 = (f32[32,512]{1,0:T(8,128)S(1)}, f32[32,512]{1,0:T(8,128)S(1)}, u32[]{:S(2)}, u32[]{:S(2)}) collective-permute-start(f32[32,512]{1,0:T(8,128)S(1)} %get-tuple-element.199), channel_id=1, source_target_pairs={{0,1},{1,0},{2,3},{3,2},{4,5},{5,4},{6,7},{7,6},{8,9},{9,8},{10,11... | collective-permute-start | bytes 196616 | tf_op jit(solution)/shard_map/ppermute | solution.py:486
  89.2 2.3 %shard_map.98 = (f32[32,384]{1,0:T(8,128)S(1)}, f32[80,128]{1,0:T(8,128)S(1)}, f32[80,128]{1,0:T(8,128)S(1)}) custom-call(s32[1]{0:T(128)S(6)} %select_n.15.core_ref.refs_0_, f32[32,2048]{1,0:T(8,128)S(1)} %get-tuple-element.201.field_ref.refs_9_.refs_10_, bf16[896,2048]{1,0:T(8,128)(2,1)S(1)} %copy-done.1, bf16[896,2048]{1,0:T(8,128)(2,1)S(1)} %copy-done.3), custom_call_target="tpu_custom_call" | custom-call | tf_op jit(solution)/shard_map/pallas_call | solution.py:83
  95.2 2.5 %collective-permute-start.35 = (f32[72,128]{1,0:T(8,128)S(1)}, f32[72,128]{1,0:T(8,128)S(1)}, u32[]{:S(2)}, u32[]{:S(2)}) collective-permute-start(f32[72,128]{1,0:T(8,128)S(1)} %get-tuple-element.211.refs_1_), channel_id=1, source_target_pairs={{0,6},{1,7},{2,4},{3,5},{4,2},{5,3},{6,0},{7,1},{8,14},{9,15},{10,... | collective-permute-start | bytes 110600 | tf_op jit(solution)/shard_map/ppermute | solution.py:486
  100.1 1.6 %collective-permute-done.34.refs_3_ = f32[72,128]{1,0:T(8,128)S(1)} collective-permute-done((f32[72,128]{1,0:T(8,128)S(1)}, f32[72,128]{1,0:T(8,128)S(1)}, u32[]{:S(2)}, u32[]{:S(2)}) %collective-permute-start.34) | collective-permute-done | bytes 36896 | tf_op jit(solution)/shard_map/ppermute | solution.py:486
  105.3 2.1 %collective-permute-start.36 = (f32[40,128]{1,0:T(8,128)S(1)}, f32[40,128]{1,0:T(8,128)S(1)}, u32[]{:S(2)}, u32[]{:S(2)}) collective-permute-start(f32[40,128]{1,0:T(8,128)S(1)} %get-tuple-element.213.refs_1_), channel_id=1, source_target_pairs={{0,8},{1,9},{2,10},{3,11},{4,12},{5,13},{6,14},{7,15},{8,0},{9,1},... | collective-permute-start | bytes 61448 | tf_op jit(solution)/shard_map/ppermute | solution.py:486
  110.7 2.2 %shard_map.103 = (f32[32,2048]{1,0:T(8,128)}, f32[32,2048]{1,0:T(8,128)}) custom-call(s32[1]{0:T(128)S(6)} %select_n.15.core_ref.refs_0_, bf16[896,2048]{1,0:T(8,128)(2,1)S(1)} %copy-done.1, bf16[896,2048]{1,0:T(8,128)(2,1)S(1)} %copy-done.3, f32[32,2048]{1,0:T(8,128)S(1)} %get-tuple-element.206.refs_3_, f32[88,128]{1,0:T(8,128)S(1)} %shard_map.102.refs_4_, ...), custom_call_target="tpu_custom_call" | custom-call | flops 1500000000 | bytes 1048576 | tf_op jit(solution)/shard_map/pallas_call | solution.py:83
  (115 shorter events, 46.4 us)
Async XLA Ops:
  8.3 21.8 %collective-permute-start.2 = (f32[40,512]{1,0:T(8,128)S(1)}, f32[40,512]{1,0:T(8,128)S(1)}, u32[]{:S(2)}, u32[]{:S(2)}) collective-permute-start(f32[40,512]{1,0:T(8,128)S(1)} %get-tuple-element.121), channel_id=1, source_target_pairs={{1,2},{3,4},{5,6},{7,8},{9,10},{11,12},{13,14},{15,16},{17,18},{19... | collective-permute-start | bytes 245768 | tf_op jit(solution)/shard_map/ppermute | solution.py:491
  9.4 12.4 %collective-permute-start.5 = (f32[72,128]{1,0:T(8,128)S(1)}, f32[72,128]{1,0:T(8,128)S(1)}, u32[]{:S(2)}, u32[]{:S(2)}) collective-permute-start(f32[72,128]{1,0:T(8,128)S(1)} %get-tuple-element.116.refs_1_), channel_id=1, source_target_pairs={{0,6},{1,7},{2,4},{3,5},{4,2},{5,3},{6,0},{7,1},{8,14},{9,15},{10,... | collective-permute-start | bytes 110600 | tf_op jit(solution)/shard_map/ppermute | solution.py:486
  14.8 7.0 %collective-permute-start.4 = (f32[72,128]{1,0:T(8,128)S(1)}, f32[72,128]{1,0:T(8,128)S(1)}, u32[]{:S(2)}, u32[]{:S(2)}) collective-permute-start(f32[72,128]{1,0:T(8,128)S(1)} %get-tuple-element.116.refs_1_), channel_id=1, source_target_pairs={{0,4},{1,5},{2,6},{3,7},{4,0},{5,1},{6,2},{7,3},{8,12},{9,13},{10,... | collective-permute-start | bytes 110600 | tf_op jit(solution)/shard_map/ppermute | solution.py:486
  14.9 7.0 %collective-permute-start.3 = (f32[72,128]{1,0:T(8,128)S(1)}, f32[72,128]{1,0:T(8,128)S(1)}, u32[]{:S(2)}, u32[]{:S(2)}) collective-permute-start(f32[72,128]{1,0:T(8,128)S(1)} %get-tuple-element.116.refs_1_), channel_id=1, source_target_pairs={{0,2},{1,3},{2,0},{3,1},{4,6},{5,7},{6,4},{7,5},{8,10},{9,11},{10,... | collective-permute-start | bytes 110600 | tf_op jit(solution)/shard_map/ppermute | solution.py:486
  16.3 13.9 %collective-permute-start.1 = (f32[40,512]{1,0:T(8,128)S(1)}, f32[40,512]{1,0:T(8,128)S(1)}, u32[]{:S(2)}, u32[]{:S(2)}) collective-permute-start(f32[40,512]{1,0:T(8,128)S(1)} %get-tuple-element.119), channel_id=1, source_target_pairs={{0,1},{1,0},{2,3},{3,2},{4,5},{5,4},{6,7},{7,6},{8,9},{9,8},{10,11... | collective-permute-start | bytes 245768 | tf_op jit(solution)/shard_map/ppermute | solution.py:486
  21.9 11.1 %collective-permute-start.8 = (f32[40,128]{1,0:T(8,128)S(1)}, f32[40,128]{1,0:T(8,128)S(1)}, u32[]{:S(2)}, u32[]{:S(2)}) collective-permute-start(f32[40,128]{1,0:T(8,128)S(1)} %get-tuple-element.128.refs_1_), channel_id=1, source_target_pairs={{0,24},{1,25},{2,26},{3,27},{4,28},{5,29},{6,30},{7,31},{8,16},{9,... | collective-permute-start | bytes 61448 | tf_op jit(solution)/shard_map/ppermute | solution.py:486
  27.0 6.1 %collective-permute-start.7 = (f32[40,128]{1,0:T(8,128)S(1)}, f32[40,128]{1,0:T(8,128)S(1)}, u32[]{:S(2)}, u32[]{:S(2)}) collective-permute-start(f32[40,128]{1,0:T(8,128)S(1)} %get-tuple-element.128.refs_1_), channel_id=1, source_target_pairs={{0,16},{1,17},{2,18},{3,19},{4,20},{5,21},{6,22},{7,23},{8,24},{9,... | collective-permute-start | bytes 61448 | tf_op jit(solution)/shard_map/ppermute | solution.py:486
  27.0 6.1 %collective-permute-start.6 = (f32[40,128]{1,0:T(8,128)S(1)}, f32[40,128]{1,0:T(8,128)S(1)}, u32[]{:S(2)}, u32[]{:S(2)}) collective-permute-start(f32[40,128]{1,0:T(8,128)S(1)} %get-tuple-element.128.refs_1_), channel_id=1, source_target_pairs={{0,8},{1,9},{2,10},{3,11},{4,12},{5,13},{6,14},{7,15},{8,0},{9,1},... | collective-permute-start | bytes 61448 | tf_op jit(solution)/shard_map/ppermute | solution.py:486
  36.5 7.1 %collective-permute-start.11 = (f32[40,512]{1,0:T(8,128)S(1)}, f32[40,512]{1,0:T(8,128)S(1)}, u32[]{:S(2)}, u32[]{:S(2)}) collective-permute-start(f32[40,512]{1,0:T(8,128)S(1)} %get-tuple-element.149), channel_id=1, source_target_pairs={{1,2},{3,4},{5,6},{7,8},{9,10},{11,12},{13,14},{15,16},{17,18},{19... | collective-permute-start | bytes 245768 | tf_op jit(solution)/shard_map/ppermute | solution.py:491
  37.3 6.2 %collective-permute-start.10 = (f32[32,512]{1,0:T(8,128)S(1)}, f32[32,512]{1,0:T(8,128)S(1)}, u32[]{:S(2)}, u32[]{:S(2)}) collective-permute-start(f32[32,512]{1,0:T(8,128)S(1)} %get-tuple-element.148), channel_id=1, source_target_pairs={{0,1},{1,0},{2,3},{3,2},{4,5},{5,4},{6,7},{7,6},{8,9},{9,8},{10,11... | collective-permute-start | bytes 196616 | tf_op jit(solution)/shard_map/ppermute | solution.py:486
  44.7 5.9 %collective-permute-start.15 = (f32[72,128]{1,0:T(8,128)S(1)}, f32[72,128]{1,0:T(8,128)S(1)}, u32[]{:S(2)}, u32[]{:S(2)}) collective-permute-start(f32[72,128]{1,0:T(8,128)S(1)} %get-tuple-element.156.refs_1_), channel_id=1, source_target_pairs={{0,6},{1,7},{2,4},{3,5},{4,2},{5,3},{6,0},{7,1},{8,14},{9,15},{10,... | collective-permute-start | bytes 110600 | tf_op jit(solution)/shard_map/ppermute | solution.py:486
  52.7 5.7 %collective-permute-start.18 = (f32[40,128]{1,0:T(8,128)S(1)}, f32[40,128]{1,0:T(8,128)S(1)}, u32[]{:S(2)}, u32[]{:S(2)}) collective-permute-start(f32[40,128]{1,0:T(8,128)S(1)} %get-tuple-element.158.refs_1_), channel_id=1, source_target_pairs={{0,24},{1,25},{2,26},{3,27},{4,28},{5,29},{6,30},{7,31},{8,16},{9,... | collective-permute-start | bytes 61448 | tf_op jit(solution)/shard_map/ppermute | solution.py:486
  56.2 4.7 %collective-permute-start.17 = (f32[40,128]{1,0:T(8,128)S(1)}, f32[40,128]{1,0:T(8,128)S(1)}, u32[]{:S(2)}, u32[]{:S(2)}) collective-permute-start(f32[40,128]{1,0:T(8,128)S(1)} %get-tuple-element.158.refs_1_), channel_id=1, source_target_pairs={{0,16},{1,17},{2,18},{3,19},{4,20},{5,21},{6,22},{7,23},{8,24},{9,... | collective-permute-start | bytes 61448 | tf_op jit(solution)/shard_map/ppermute | solution.py:486
  56.2 4.7 %collective-permute-start.16 = (f32[40,128]{1,0:T(8,128)S(1)}, f32[40,128]{1,0:T(8,128)S(1)}, u32[]{:S(2)}, u32[]{:S(2)}) collective-permute-start(f32[40,128]{1,0:T(8,128)S(1)} %get-tuple-element.158.refs_1_), channel_id=1, source_target_pairs={{0,8},{1,9},{2,10},{3,11},{4,12},{5,13},{6,14},{7,15},{8,0},{9,1},... | collective-permute-start | bytes 61448 | tf_op jit(solution)/shard_map/ppermute | solution.py:486
  66.4 14.1 %collective-permute-start.28 = (f32[40,512]{1,0:T(8,128)S(1)}, f32[40,512]{1,0:T(8,128)S(1)}, u32[]{:S(2)}, u32[]{:S(2)}) collective-permute-start(f32[40,512]{1,0:T(8,128)S(1)} %get-tuple-element.178), channel_id=1, source_target_pairs={{1,2},{3,4},{5,6},{7,8},{9,10},{11,12},{13,14},{15,16},{17,18},{19... | collective-permute-start | bytes 245768 | tf_op jit(solution)/shard_map/ppermute | solution.py:491
  67.1 13.4 %collective-permute-start.27 = (f32[32,512]{1,0:T(8,128)S(1)}, f32[32,512]{1,0:T(8,128)S(1)}, u32[]{:S(2)}, u32[]{:S(2)}) collective-permute-start(f32[32,512]{1,0:T(8,128)S(1)} %get-tuple-element.177), channel_id=1, source_target_pairs={{0,1},{1,0},{2,3},{3,2},{4,5},{5,4},{6,7},{7,6},{8,9},{9,8},{10,11... | collective-permute-start | bytes 196616 | tf_op jit(solution)/shard_map/ppermute | solution.py:486
  68.9 6.0 %collective-permute-start.23 = (f32[72,128]{1,0:T(8,128)S(1)}, f32[72,128]{1,0:T(8,128)S(1)}, u32[]{:S(2)}, u32[]{:S(2)}) collective-permute-start(f32[72,128]{1,0:T(8,128)S(1)} %get-tuple-element.171.refs_1_), channel_id=1, source_target_pairs={{0,6},{1,7},{2,4},{3,5},{4,2},{5,3},{6,0},{7,1},{8,14},{9,15},{10,... | collective-permute-start | bytes 110600 | tf_op jit(solution)/shard_map/ppermute | solution.py:486
  76.0 5.6 %collective-permute-start.26 = (f32[40,128]{1,0:T(8,128)S(1)}, f32[40,128]{1,0:T(8,128)S(1)}, u32[]{:S(2)}, u32[]{:S(2)}) collective-permute-start(f32[40,128]{1,0:T(8,128)S(1)} %get-tuple-element.176.refs_1_), channel_id=1, source_target_pairs={{0,24},{1,25},{2,26},{3,27},{4,28},{5,29},{6,30},{7,31},{8,16},{9,... | collective-permute-start | bytes 61448 | tf_op jit(solution)/shard_map/ppermute | solution.py:486
  79.0 4.7 %collective-permute-start.25 = (f32[40,128]{1,0:T(8,128)S(1)}, f32[40,128]{1,0:T(8,128)S(1)}, u32[]{:S(2)}, u32[]{:S(2)}) collective-permute-start(f32[40,128]{1,0:T(8,128)S(1)} %get-tuple-element.176.refs_1_), channel_id=1, source_target_pairs={{0,16},{1,17},{2,18},{3,19},{4,20},{5,21},{6,22},{7,23},{8,24},{9,... | collective-permute-start | bytes 61448 | tf_op jit(solution)/shard_map/ppermute | solution.py:486
  86.4 7.6 %collective-permute-start.31 = (f32[40,512]{1,0:T(8,128)S(1)}, f32[40,512]{1,0:T(8,128)S(1)}, u32[]{:S(2)}, u32[]{:S(2)}) collective-permute-start(f32[40,512]{1,0:T(8,128)S(1)} %get-tuple-element.200), channel_id=1, source_target_pairs={{1,2},{3,4},{5,6},{7,8},{9,10},{11,12},{13,14},{15,16},{17,18},{19... | collective-permute-start | bytes 245768 | tf_op jit(solution)/shard_map/ppermute | solution.py:491
  87.3 6.7 %collective-permute-start.30 = (f32[32,512]{1,0:T(8,128)S(1)}, f32[32,512]{1,0:T(8,128)S(1)}, u32[]{:S(2)}, u32[]{:S(2)}) collective-permute-start(f32[32,512]{1,0:T(8,128)S(1)} %get-tuple-element.199), channel_id=1, source_target_pairs={{0,1},{1,0},{2,3},{3,2},{4,5},{5,4},{6,7},{7,6},{8,9},{9,8},{10,11... | collective-permute-start | bytes 196616 | tf_op jit(solution)/shard_map/ppermute | solution.py:486
  95.2 4.9 %collective-permute-start.35 = (f32[72,128]{1,0:T(8,128)S(1)}, f32[72,128]{1,0:T(8,128)S(1)}, u32[]{:S(2)}, u32[]{:S(2)}) collective-permute-start(f32[72,128]{1,0:T(8,128)S(1)} %get-tuple-element.211.refs_1_), channel_id=1, source_target_pairs={{0,6},{1,7},{2,4},{3,5},{4,2},{5,3},{6,0},{7,1},{8,14},{9,15},{10,... | collective-permute-start | bytes 110600 | tf_op jit(solution)/shard_map/ppermute | solution.py:486
  103.0 5.6 %collective-permute-start.38 = (f32[40,128]{1,0:T(8,128)S(1)}, f32[40,128]{1,0:T(8,128)S(1)}, u32[]{:S(2)}, u32[]{:S(2)}) collective-permute-start(f32[40,128]{1,0:T(8,128)S(1)} %get-tuple-element.213.refs_1_), channel_id=1, source_target_pairs={{0,24},{1,25},{2,26},{3,27},{4,28},{5,29},{6,30},{7,31},{8,16},{9,... | collective-permute-start | bytes 61448 | tf_op jit(solution)/shard_map/ppermute | solution.py:486
  104.1 4.7 %collective-permute-start.37 = (f32[40,128]{1,0:T(8,128)S(1)}, f32[40,128]{1,0:T(8,128)S(1)}, u32[]{:S(2)}, u32[]{:S(2)}) collective-permute-start(f32[40,128]{1,0:T(8,128)S(1)} %get-tuple-element.213.refs_1_), channel_id=1, source_target_pairs={{0,16},{1,17},{2,18},{3,19},{4,20},{5,21},{6,22},{7,23},{8,24},{9,... | collective-permute-start | bytes 61448 | tf_op jit(solution)/shard_map/ppermute | solution.py:486
  (24 other events, 79.9 us)

commit v2 on v1

--- a/solution.py
+++ b/solution.py
@@ -169,8 +169,18 @@
     return chosen(core, head, tail), chosen(core, tail, head)
 
 
-def edges_kernel(core_ref, field_ref, lane_ref, paired_ref, other_ref):
+def edges_kernel(place_ref, core_ref, ids_ref, field_ref, lane_ref, paired_ref, other_ref, weights_ref):
     core = core_ref[0]
+    leaves = ids_ref.shape[0]
+    for leaf in range(leaves):
+        for offset in range(-1, WIN - 1):
+            target = place_ref[0] * leaves + leaf + offset
+            found = ids_ref[leaf, 0] == target
+            for slot in range(1, WIN):
+                found = jnp.logical_or(found, ids_ref[leaf, slot] == target)
+            value = jnp.where(jnp.logical_and(found, target >= 0), 1.0 / (16 * WIN), 0.0)
+            at = WIN * leaf + offset + 1
+            weights_ref[at : at + 1] = jnp.full((1, LEAF), value, jnp.float32)
     for ref, field, place in zip((paired_ref, other_ref), sides(core, field_ref), sides(core, lane_ref)):
         ref[...] = jnp.concatenate([field, place], axis=0)
 
@@ -204,13 +214,6 @@
 def weight_of(weights_ref, leaf, offset):
     at = WIN * leaf + offset + 1
     return weights_ref[at : at + 1]
-
-
-def leaf_weights(near_ids, first_leaf):
-    target = first_leaf + jnp.arange(near_ids.shape[0])[:, None] + jnp.arange(WIN)[None, :] - 1
-    found = jnp.any(near_ids[:, None, :] == target[:, :, None], axis=2) & (target >= 0)
-    weights = jnp.where(found, 1.0 / (16 * WIN), 0.0).astype(jnp.float32)
-    return jnp.broadcast_to(weights.reshape(-1, 1), (weights.size, LEAF))
 
 
 def row_groups(leaves):
@@ -477,7 +480,6 @@
     place = jnp.reshape(lax.axis_index(BOTH), (1,))
     core = place % 2
     nugget = nugget[None, :]
-    weights = leaf_weights(near_ids, place[0] * leaves)
 
     stages = [list(range(bit, min(bit + 2, crossing))) for bit in range(1, crossing, 2)]
     siblings = sum(len(bits) == 2 for bits in stages)
@@ -563,7 +565,8 @@
         compiler_params=pltpu.CompilerParams(vmem_limit_bytes=44 * 2**20),
         cost_estimate=pl.CostEstimate(flops=FLOPS, bytes_accessed=2**20, transcendentals=0),
     )(coords, basis)
-    edges = call(edges_kernel, [f32(rows + 8, LEAF)] * 2, core, rhs, lanes, scalars=1)
+    shapes = [f32(rows + 8, LEAF)] * 2 + [f32(WIN * leaves, LEAF)]
+    *edges, weights = call(edges_kernel, shapes, place, core, near_ids, rhs, lanes, scalars=3)
     back_matrices = outside = None
 
     def after(message, *values):

time: 113 us -> 112 us (level)
  local copies, waits for them, and re-layouts: 2.26 us -> 0.76 us
    unnamed x16 -> x8, local copies, waits for them, and re-layouts: 2.01 us -> 0.76 us
  transfers between devices with their start and end apart: 40 -> 40, of which waited for: 17 -> 17; matrix products, arithmetic and copies ran while one was open for 0% -> 0% of each run, Pallas kernels for 23% -> 24%
where the time goes in v2:
time: 112 us
  starting transfers between devices  46.9 us (42%)
  Pallas kernels  42.7 us (38%)
  waiting for transfers between devices  20.4 us (18%)
    ppermute x36, starting transfers between devices, swap(): lax.ppermute(value, BOTH, [(source, source ^ mask) for source in range(de...  43.8 us
    pallas_call x35, Pallas kernels, call(): pl.pallas_call(body, out_shape=outs, in_specs=[whole(pltpu.SMEM)] * scala...  39.2 us
    ppermute x36, waiting for transfers between devices, swap(): lax.ppermute(value, BOTH, [(source, source ^ mask) for source in range(de...  20.4 us
    pallas_call x1, Pallas kernels, per_device(): pl.pallas_call(functools.partial(setup_kernel, groups[:1]), out_shape=[bf...  3.48 us
    ppermute x4, starting transfers between devices, far_halo(): lax.ppermute(other, BOTH, outward + [(target, source) for source, target...  3.05 us
  transfers between devices with their start and end apart: 40, of which 17 were waited for; matrix products, arithmetic and copies ran while one was open for 0% of the time, Pallas kernels for 24%

profile of v2, /device:TPU:0, one launch (start us, length us, event | category | flops | bytes accessed | tf_op | source)
XLA Modules:
  0.0 111.8 jit_solution(15175644189538915981)
XLA Ops:
  1.4 3.5 %shard_map.68 = (bf16[2,512,512]{2,1,0:T(8,128)(2,1)S(1)}, bf16[2,512,512]{2,1,0:T(8,128)(2,1)S(1)}, bf16[896,2048]{1,0:T(8,128)(2,1)S(1)}, bf16[896,2048]{1,0:T(8,128)(2,1)S(1)}, f32[8,2048]{1,0:T(8,128)S(1)}) custom-call(f32[3,2048]{1,0:T(4,128)S(1)} %copy-done.3, f32[7,128,2048]{2,1,0:T(8,128)} %basis_ref.1), custom_call_target="tpu_custom_call" | custom-call | flops 3000000000 | bytes 1048576 | tf_op jit(solution)/shard_map/pallas_call | solution.py:557
  4.9 2.3 %shard_map.70 = (f32[32,384]{1,0:T(8,128)S(1)}, f32[80,128]{1,0:T(8,128)S(1)}, f32[80,128]{1,0:T(8,128)S(1)}, f32[8,128]{1,0:T(8,128)S(1)}) custom-call(s32[1]{0:T(128)S(6)} %select_n.7.core_ref.refs_0_, f32[32,2048]{1,0:T(8,128)S(1)} %copy-done, bf16[896,2048]{1,0:T(8,128)(2,1)S(1)} %get-tuple-element.112.high_ref.refs_1_, ...), custom_call_target="tpu_custom_call" | custom-call | flops 3000000000 | bytes 1048576 | tf_op jit(solution)/shard_map/pallas_call | solution.py:83
  9.1 5.4 %collective-permute-start.5 = (f32[72,128]{1,0:T(8,128)S(1)}, f32[72,128]{1,0:T(8,128)S(1)}, u32[]{:S(2)}, u32[]{:S(2)}) collective-permute-start(f32[72,128]{1,0:T(8,128)S(1)} %get-tuple-element.119.refs_1_), channel_id=1, source_target_pairs={{0,6},{1,7},{2,4},{3,5},{4,2},{5,3},{6,0},{7,1},{8,14},{9,15},{10,... | collective-permute-start | bytes 110600 | tf_op jit(solution)/shard_map/ppermute | solution.py:488
  15.9 5.6 %shard_map.72 = (bf16[5,512,512]{2,1,0:T(8,128)(2,1)S(1)}, bf16[5,512,512]{2,1,0:T(8,128)(2,1)S(1)}) custom-call(f32[8,2048]{1,0:T(8,128)S(1)} %get-tuple-element.131.lane_ref.refs_0_), custom_call_target="tpu_custom_call" | custom-call | flops 6000000000 | bytes 1048576 | tf_op jit(solution)/shard_map/pallas_call | solution.py:83
  21.5 5.1 %collective-permute-start.8 = (f32[40,128]{1,0:T(8,128)S(1)}, f32[40,128]{1,0:T(8,128)S(1)}, u32[]{:S(2)}, u32[]{:S(2)}) collective-permute-start(f32[40,128]{1,0:T(8,128)S(1)} %get-tuple-element.130.refs_1_), channel_id=1, source_target_pairs={{0,24},{1,25},{2,26},{3,27},{4,28},{5,29},{6,30},{7,31},{8,16},{9,... | collective-permute-start | bytes 61448 | tf_op jit(solution)/shard_map/ppermute | solution.py:488
  29.7 2.9 %shard_map.74 = (bf16[2,512,512]{2,1,0:T(8,128)(2,1)S(1)}, bf16[2,512,512]{2,1,0:T(8,128)(2,1)S(1)}) custom-call(s32[1]{0:T(128)S(6)} %select_n.7.core_ref.refs_0_, f32[8,2048]{1,0:T(8,128)S(1)} %get-tuple-element.131.lane_ref.refs_0_, f32[40,512]{1,0:T(8,128)S(1)} %collective-permute-done.1.refs_1_.refs_2_, f32[40,512]{1,0:T(8,128)S(1)} %collective-permute-done.2.refs_2_.refs_3_), custom_call_target="tpu_custom_call" | custom-call | flops 3000000000 | bytes 1048576 | tf_op jit(solution)/shard_map/pallas_call | solution.py:83
  36.2 1.5 %collective-permute-start.10 = (f32[32,512]{1,0:T(8,128)S(1)}, f32[32,512]{1,0:T(8,128)S(1)}, u32[]{:S(2)}, u32[]{:S(2)}) collective-permute-start(f32[32,512]{1,0:T(8,128)S(1)} %get-tuple-element.150), channel_id=1, source_target_pairs={{0,1},{1,0},{2,3},{3,2},{4,5},{5,4},{6,7},{7,6},{8,9},{9,8},{10,11... | collective-permute-start | bytes 196616 | tf_op jit(solution)/shard_map/ppermute | solution.py:488
  37.7 2.3 %shard_map.82 = (f32[32,384]{1,0:T(8,128)S(1)}, f32[80,128]{1,0:T(8,128)S(1)}, f32[80,128]{1,0:T(8,128)S(1)}) custom-call(s32[1]{0:T(128)S(6)} %select_n.7.core_ref.refs_0_, f32[32,2048]{1,0:T(8,128)S(1)} %get-tuple-element.152.field_ref.refs_9_.refs_11_.refs_8_.refs_10_, bf16[896,2048]{1,0:T(8,128)(2,1)S(1)} %get-tuple-element.112.high_ref.refs_1_, ...), custom_call_target="tpu_custom_call" | custom-call | tf_op jit(solution)/shard_map/pallas_call | solution.py:83
  43.6 3.7 %collective-permute-start.15 = (f32[72,128]{1,0:T(8,128)S(1)}, f32[72,128]{1,0:T(8,128)S(1)}, u32[]{:S(2)}, u32[]{:S(2)}) collective-permute-start(f32[72,128]{1,0:T(8,128)S(1)} %get-tuple-element.158.refs_1_), channel_id=1, source_target_pairs={{0,6},{1,7},{2,4},{3,5},{4,2},{5,3},{6,0},{7,1},{8,14},{9,15},{10,... | collective-permute-start | bytes 110600 | tf_op jit(solution)/shard_map/ppermute | solution.py:488
  48.0 1.5 %collective-permute-done.15.refs_4_ = f32[72,128]{1,0:T(8,128)S(1)} collective-permute-done((f32[72,128]{1,0:T(8,128)S(1)}, f32[72,128]{1,0:T(8,128)S(1)}, u32[]{:S(2)}, u32[]{:S(2)}) %collective-permute-start.15) | collective-permute-done | bytes 36896 | tf_op jit(solution)/shard_map/ppermute | solution.py:488
  49.5 1.8 %collective-permute-done.14.refs_3_ = f32[72,128]{1,0:T(8,128)S(1)} collective-permute-done((f32[72,128]{1,0:T(8,128)S(1)}, f32[72,128]{1,0:T(8,128)S(1)}, u32[]{:S(2)}, u32[]{:S(2)}) %collective-permute-start.14) | collective-permute-done | bytes 36896 | tf_op jit(solution)/shard_map/ppermute | solution.py:488
  51.6 3.6 %collective-permute-start.18 = (f32[40,128]{1,0:T(8,128)S(1)}, f32[40,128]{1,0:T(8,128)S(1)}, u32[]{:S(2)}, u32[]{:S(2)}) collective-permute-start(f32[40,128]{1,0:T(8,128)S(1)} %get-tuple-element.160.refs_1_), channel_id=1, source_target_pairs={{0,24},{1,25},{2,26},{3,27},{4,28},{5,29},{6,30},{7,31},{8,16},{9,... | collective-permute-start | bytes 61448 | tf_op jit(solution)/shard_map/ppermute | solution.py:488
  57.2 2.7 %collective-permute-done.17.refs_3_ = f32[40,128]{1,0:T(8,128)S(1)} collective-permute-done((f32[40,128]{1,0:T(8,128)S(1)}, f32[40,128]{1,0:T(8,128)S(1)}, u32[]{:S(2)}, u32[]{:S(2)}) %collective-permute-start.17) | collective-permute-done | bytes 20512 | tf_op jit(solution)/shard_map/ppermute | solution.py:488
  62.8 2.3 %shard_map.88 = (f32[32,384]{1,0:T(8,128)S(1)}, f32[80,128]{1,0:T(8,128)S(1)}, f32[80,128]{1,0:T(8,128)S(1)}, f32[8,128]{1,0:T(8,128)S(1)}) custom-call(s32[1]{0:T(128)S(6)} %select_n.7.core_ref.refs_0_, f32[32,2048]{1,0:T(8,128)S(1)} %get-tuple-element.174.field_ref.refs_7_.refs_8_, bf16[896,2048]{1,0:T(8,128)(2,1)S(1)} %get-tuple-element.112.high_ref.refs_1_, ...), custom_call_target="tpu_custom_call" | custom-call | tf_op jit(solution)/shard_map/pallas_call | solution.py:83
  66.0 1.8 %collective-permute-start.27 = (f32[32,512]{1,0:T(8,128)S(1)}, f32[32,512]{1,0:T(8,128)S(1)}, u32[]{:S(2)}, u32[]{:S(2)}) collective-permute-start(f32[32,512]{1,0:T(8,128)S(1)} %get-tuple-element.179), channel_id=1, source_target_pairs={{0,1},{1,0},{2,3},{3,2},{4,5},{5,4},{6,7},{7,6},{8,9},{9,8},{10,11... | collective-permute-start | bytes 196616 | tf_op jit(solution)/shard_map/ppermute | solution.py:488
  67.8 1.9 %collective-permute-start.23 = (f32[72,128]{1,0:T(8,128)S(1)}, f32[72,128]{1,0:T(8,128)S(1)}, u32[]{:S(2)}, u32[]{:S(2)}) collective-permute-start(f32[72,128]{1,0:T(8,128)S(1)} %get-tuple-element.173.refs_1_), channel_id=1, source_target_pairs={{0,6},{1,7},{2,4},{3,5},{4,2},{5,3},{6,0},{7,1},{8,14},{9,15},{10,... | collective-permute-start | bytes 110600 | tf_op jit(solution)/shard_map/ppermute | solution.py:488
  75.1 2.7 %collective-permute-start.26 = (f32[40,128]{1,0:T(8,128)S(1)}, f32[40,128]{1,0:T(8,128)S(1)}, u32[]{:S(2)}, u32[]{:S(2)}) collective-permute-start(f32[40,128]{1,0:T(8,128)S(1)} %get-tuple-element.178.refs_1_), channel_id=1, source_target_pairs={{0,24},{1,25},{2,26},{3,27},{4,28},{5,29},{6,30},{7,31},{8,16},{9,... | collective-permute-start | bytes 61448 | tf_op jit(solution)/shard_map/ppermute | solution.py:488
  78.0 1.6 %collective-permute-start.24 = (f32[40,128]{1,0:T(8,128)S(1)}, f32[40,128]{1,0:T(8,128)S(1)}, u32[]{:S(2)}, u32[]{:S(2)}) collective-permute-start(f32[40,128]{1,0:T(8,128)S(1)} %get-tuple-element.178.refs_1_), channel_id=1, source_target_pairs={{0,8},{1,9},{2,10},{3,11},{4,12},{5,13},{6,14},{7,15},{8,0},{9,1},... | collective-permute-start | bytes 61448 | tf_op jit(solution)/shard_map/ppermute | solution.py:488
  80.8 1.7 %collective-permute-done.25.refs_3_ = f32[40,128]{1,0:T(8,128)S(1)} collective-permute-done((f32[40,128]{1,0:T(8,128)S(1)}, f32[40,128]{1,0:T(8,128)S(1)}, u32[]{:S(2)}, u32[]{:S(2)}) %collective-permute-start.25) | collective-permute-done | bytes 20512 | tf_op jit(solution)/shard_map/ppermute | solution.py:488
  86.2 2.3 %collective-permute-start.30 = (f32[32,512]{1,0:T(8,128)S(1)}, f32[32,512]{1,0:T(8,128)S(1)}, u32[]{:S(2)}, u32[]{:S(2)}) collective-permute-start(f32[32,512]{1,0:T(8,128)S(1)} %get-tuple-element.201), channel_id=1, source_target_pairs={{0,1},{1,0},{2,3},{3,2},{4,5},{5,4},{6,7},{7,6},{8,9},{9,8},{10,11... | collective-permute-start | bytes 196616 | tf_op jit(solution)/shard_map/ppermute | solution.py:488
  88.5 2.3 %shard_map.98 = (f32[32,384]{1,0:T(8,128)S(1)}, f32[80,128]{1,0:T(8,128)S(1)}, f32[80,128]{1,0:T(8,128)S(1)}) custom-call(s32[1]{0:T(128)S(6)} %select_n.7.core_ref.refs_0_, f32[32,2048]{1,0:T(8,128)S(1)} %get-tuple-element.203.field_ref.refs_9_.refs_10_, bf16[896,2048]{1,0:T(8,128)(2,1)S(1)} %get-tuple-element.112.high_ref.refs_1_, ...), custom_call_target="tpu_custom_call" | custom-call | tf_op jit(solution)/shard_map/pallas_call | solution.py:83
  94.5 2.3 %collective-permute-start.35 = (f32[72,128]{1,0:T(8,128)S(1)}, f32[72,128]{1,0:T(8,128)S(1)}, u32[]{:S(2)}, u32[]{:S(2)}) collective-permute-start(f32[72,128]{1,0:T(8,128)S(1)} %get-tuple-element.213.refs_1_), channel_id=1, source_target_pairs={{0,6},{1,7},{2,4},{3,5},{4,2},{5,3},{6,0},{7,1},{8,14},{9,15},{10,... | collective-permute-start | bytes 110600 | tf_op jit(solution)/shard_map/ppermute | solution.py:488
  104.2 2.1 %collective-permute-start.36 = (f32[40,128]{1,0:T(8,128)S(1)}, f32[40,128]{1,0:T(8,128)S(1)}, u32[]{:S(2)}, u32[]{:S(2)}) collective-permute-start(f32[40,128]{1,0:T(8,128)S(1)} %get-tuple-element.215.refs_1_), channel_id=1, source_target_pairs={{0,8},{1,9},{2,10},{3,11},{4,12},{5,13},{6,14},{7,15},{8,0},{9,1},... | collective-permute-start | bytes 61448 | tf_op jit(solution)/shard_map/ppermute | solution.py:488
  109.6 2.2 %shard_map.103 = (f32[32,2048]{1,0:T(8,128)}, f32[32,2048]{1,0:T(8,128)}) custom-call(s32[1]{0:T(128)S(6)} %select_n.7.core_ref.refs_0_, bf16[896,2048]{1,0:T(8,128)(2,1)S(1)} %get-tuple-element.112.high_ref.refs_1_, bf16[896,2048]{1,0:T(8,128)(2,1)S(1)} %get-tuple-element.113.low_ref.refs_2_, f32[32,2048]{1,0:T(8,128)S(1)} %get-tuple-element.208.refs_3_, ...), custom_call_target="tpu_custom_call" | custom-call | flops 1500000000 | bytes 1048576 | tf_op jit(solution)/shard_map/pallas_call | solution.py:83
  (100 shorter events, 45.5 us)
Async XLA Ops:
  8.4 21.3 %collective-permute-start.2 = (f32[40,512]{1,0:T(8,128)S(1)}, f32[40,512]{1,0:T(8,128)S(1)}, u32[]{:S(2)}, u32[]{:S(2)}) collective-permute-start(f32[40,512]{1,0:T(8,128)S(1)} %get-tuple-element.123), channel_id=1, source_target_pairs={{1,2},{3,4},{5,6},{7,8},{9,10},{11,12},{13,14},{15,16},{17,18},{19... | collective-permute-start | bytes 245768 | tf_op jit(solution)/shard_map/ppermute | solution.py:493
  9.1 12.4 %collective-permute-start.5 = (f32[72,128]{1,0:T(8,128)S(1)}, f32[72,128]{1,0:T(8,128)S(1)}, u32[]{:S(2)}, u32[]{:S(2)}) collective-permute-start(f32[72,128]{1,0:T(8,128)S(1)} %get-tuple-element.119.refs_1_), channel_id=1, source_target_pairs={{0,6},{1,7},{2,4},{3,5},{4,2},{5,3},{6,0},{7,1},{8,14},{9,15},{10,... | collective-permute-start | bytes 110600 | tf_op jit(solution)/shard_map/ppermute | solution.py:488
  14.5 7.0 %collective-permute-start.4 = (f32[72,128]{1,0:T(8,128)S(1)}, f32[72,128]{1,0:T(8,128)S(1)}, u32[]{:S(2)}, u32[]{:S(2)}) collective-permute-start(f32[72,128]{1,0:T(8,128)S(1)} %get-tuple-element.119.refs_1_), channel_id=1, source_target_pairs={{0,4},{1,5},{2,6},{3,7},{4,0},{5,1},{6,2},{7,3},{8,12},{9,13},{10,... | collective-permute-start | bytes 110600 | tf_op jit(solution)/shard_map/ppermute | solution.py:488
  14.5 7.0 %collective-permute-start.3 = (f32[72,128]{1,0:T(8,128)S(1)}, f32[72,128]{1,0:T(8,128)S(1)}, u32[]{:S(2)}, u32[]{:S(2)}) collective-permute-start(f32[72,128]{1,0:T(8,128)S(1)} %get-tuple-element.119.refs_1_), channel_id=1, source_target_pairs={{0,2},{1,3},{2,0},{3,1},{4,6},{5,7},{6,4},{7,5},{8,10},{9,11},{10,... | collective-permute-start | bytes 110600 | tf_op jit(solution)/shard_map/ppermute | solution.py:488
  15.9 13.8 %collective-permute-start.1 = (f32[40,512]{1,0:T(8,128)S(1)}, f32[40,512]{1,0:T(8,128)S(1)}, u32[]{:S(2)}, u32[]{:S(2)}) collective-permute-start(f32[40,512]{1,0:T(8,128)S(1)} %get-tuple-element.121), channel_id=1, source_target_pairs={{0,1},{1,0},{2,3},{3,2},{4,5},{5,4},{6,7},{7,6},{8,9},{9,8},{10,11... | collective-permute-start | bytes 245768 | tf_op jit(solution)/shard_map/ppermute | solution.py:488
  21.5 11.1 %collective-permute-start.8 = (f32[40,128]{1,0:T(8,128)S(1)}, f32[40,128]{1,0:T(8,128)S(1)}, u32[]{:S(2)}, u32[]{:S(2)}) collective-permute-start(f32[40,128]{1,0:T(8,128)S(1)} %get-tuple-element.130.refs_1_), channel_id=1, source_target_pairs={{0,24},{1,25},{2,26},{3,27},{4,28},{5,29},{6,30},{7,31},{8,16},{9,... | collective-permute-start | bytes 61448 | tf_op jit(solution)/shard_map/ppermute | solution.py:488
  26.6 6.0 %collective-permute-start.7 = (f32[40,128]{1,0:T(8,128)S(1)}, f32[40,128]{1,0:T(8,128)S(1)}, u32[]{:S(2)}, u32[]{:S(2)}) collective-permute-start(f32[40,128]{1,0:T(8,128)S(1)} %get-tuple-element.130.refs_1_), channel_id=1, source_target_pairs={{0,16},{1,17},{2,18},{3,19},{4,20},{5,21},{6,22},{7,23},{8,24},{9,... | collective-permute-start | bytes 61448 | tf_op jit(solution)/shard_map/ppermute | solution.py:488
  26.6 6.0 %collective-permute-start.6 = (f32[40,128]{1,0:T(8,128)S(1)}, f32[40,128]{1,0:T(8,128)S(1)}, u32[]{:S(2)}, u32[]{:S(2)}) collective-permute-start(f32[40,128]{1,0:T(8,128)S(1)} %get-tuple-element.130.refs_1_), channel_id=1, source_target_pairs={{0,8},{1,9},{2,10},{3,11},{4,12},{5,13},{6,14},{7,15},{8,0},{9,1},... | collective-permute-start | bytes 61448 | tf_op jit(solution)/shard_map/ppermute | solution.py:488
  35.3 7.1 %collective-permute-start.11 = (f32[40,512]{1,0:T(8,128)S(1)}, f32[40,512]{1,0:T(8,128)S(1)}, u32[]{:S(2)}, u32[]{:S(2)}) collective-permute-start(f32[40,512]{1,0:T(8,128)S(1)} %get-tuple-element.151), channel_id=1, source_target_pairs={{1,2},{3,4},{5,6},{7,8},{9,10},{11,12},{13,14},{15,16},{17,18},{19... | collective-permute-start | bytes 245768 | tf_op jit(solution)/shard_map/ppermute | solution.py:493
  36.2 6.3 %collective-permute-start.10 = (f32[32,512]{1,0:T(8,128)S(1)}, f32[32,512]{1,0:T(8,128)S(1)}, u32[]{:S(2)}, u32[]{:S(2)}) collective-permute-start(f32[32,512]{1,0:T(8,128)S(1)} %get-tuple-element.150), channel_id=1, source_target_pairs={{0,1},{1,0},{2,3},{3,2},{4,5},{5,4},{6,7},{7,6},{8,9},{9,8},{10,11... | collective-permute-start | bytes 196616 | tf_op jit(solution)/shard_map/ppermute | solution.py:488
  43.6 5.9 %collective-permute-start.15 = (f32[72,128]{1,0:T(8,128)S(1)}, f32[72,128]{1,0:T(8,128)S(1)}, u32[]{:S(2)}, u32[]{:S(2)}) collective-permute-start(f32[72,128]{1,0:T(8,128)S(1)} %get-tuple-element.158.refs_1_), channel_id=1, source_target_pairs={{0,6},{1,7},{2,4},{3,5},{4,2},{5,3},{6,0},{7,1},{8,14},{9,15},{10,... | collective-permute-start | bytes 110600 | tf_op jit(solution)/shard_map/ppermute | solution.py:488
  51.6 5.7 %collective-permute-start.18 = (f32[40,128]{1,0:T(8,128)S(1)}, f32[40,128]{1,0:T(8,128)S(1)}, u32[]{:S(2)}, u32[]{:S(2)}) collective-permute-start(f32[40,128]{1,0:T(8,128)S(1)} %get-tuple-element.160.refs_1_), channel_id=1, source_target_pairs={{0,24},{1,25},{2,26},{3,27},{4,28},{5,29},{6,30},{7,31},{8,16},{9,... | collective-permute-start | bytes 61448 | tf_op jit(solution)/shard_map/ppermute | solution.py:488
  55.2 4.7 %collective-permute-start.17 = (f32[40,128]{1,0:T(8,128)S(1)}, f32[40,128]{1,0:T(8,128)S(1)}, u32[]{:S(2)}, u32[]{:S(2)}) collective-permute-start(f32[40,128]{1,0:T(8,128)S(1)} %get-tuple-element.160.refs_1_), channel_id=1, source_target_pairs={{0,16},{1,17},{2,18},{3,19},{4,20},{5,21},{6,22},{7,23},{8,24},{9,... | collective-permute-start | bytes 61448 | tf_op jit(solution)/shard_map/ppermute | solution.py:488
  55.2 4.7 %collective-permute-start.16 = (f32[40,128]{1,0:T(8,128)S(1)}, f32[40,128]{1,0:T(8,128)S(1)}, u32[]{:S(2)}, u32[]{:S(2)}) collective-permute-start(f32[40,128]{1,0:T(8,128)S(1)} %get-tuple-element.160.refs_1_), channel_id=1, source_target_pairs={{0,8},{1,9},{2,10},{3,11},{4,12},{5,13},{6,14},{7,15},{8,0},{9,1},... | collective-permute-start | bytes 61448 | tf_op jit(solution)/shard_map/ppermute | solution.py:488
  65.4 14.2 %collective-permute-start.28 = (f32[40,512]{1,0:T(8,128)S(1)}, f32[40,512]{1,0:T(8,128)S(1)}, u32[]{:S(2)}, u32[]{:S(2)}) collective-permute-start(f32[40,512]{1,0:T(8,128)S(1)} %get-tuple-element.180), channel_id=1, source_target_pairs={{1,2},{3,4},{5,6},{7,8},{9,10},{11,12},{13,14},{15,16},{17,18},{19... | collective-permute-start | bytes 245768 | tf_op jit(solution)/shard_map/ppermute | solution.py:493
  66.0 13.6 %collective-permute-start.27 = (f32[32,512]{1,0:T(8,128)S(1)}, f32[32,512]{1,0:T(8,128)S(1)}, u32[]{:S(2)}, u32[]{:S(2)}) collective-permute-start(f32[32,512]{1,0:T(8,128)S(1)} %get-tuple-element.179), channel_id=1, source_target_pairs={{0,1},{1,0},{2,3},{3,2},{4,5},{5,4},{6,7},{7,6},{8,9},{9,8},{10,11... | collective-permute-start | bytes 196616 | tf_op jit(solution)/shard_map/ppermute | solution.py:488
  67.8 6.0 %collective-permute-start.23 = (f32[72,128]{1,0:T(8,128)S(1)}, f32[72,128]{1,0:T(8,128)S(1)}, u32[]{:S(2)}, u32[]{:S(2)}) collective-permute-start(f32[72,128]{1,0:T(8,128)S(1)} %get-tuple-element.173.refs_1_), channel_id=1, source_target_pairs={{0,6},{1,7},{2,4},{3,5},{4,2},{5,3},{6,0},{7,1},{8,14},{9,15},{10,... | collective-permute-start | bytes 110600 | tf_op jit(solution)/shard_map/ppermute | solution.py:488
  75.1 5.6 %collective-permute-start.26 = (f32[40,128]{1,0:T(8,128)S(1)}, f32[40,128]{1,0:T(8,128)S(1)}, u32[]{:S(2)}, u32[]{:S(2)}) collective-permute-start(f32[40,128]{1,0:T(8,128)S(1)} %get-tuple-element.178.refs_1_), channel_id=1, source_target_pairs={{0,24},{1,25},{2,26},{3,27},{4,28},{5,29},{6,30},{7,31},{8,16},{9,... | collective-permute-start | bytes 61448 | tf_op jit(solution)/shard_map/ppermute | solution.py:488
  77.8 4.7 %collective-permute-start.25 = (f32[40,128]{1,0:T(8,128)S(1)}, f32[40,128]{1,0:T(8,128)S(1)}, u32[]{:S(2)}, u32[]{:S(2)}) collective-permute-start(f32[40,128]{1,0:T(8,128)S(1)} %get-tuple-element.178.refs_1_), channel_id=1, source_target_pairs={{0,16},{1,17},{2,18},{3,19},{4,20},{5,21},{6,22},{7,23},{8,24},{9,... | collective-permute-start | bytes 61448 | tf_op jit(solution)/shard_map/ppermute | solution.py:488
  85.3 8.0 %collective-permute-start.31 = (f32[40,512]{1,0:T(8,128)S(1)}, f32[40,512]{1,0:T(8,128)S(1)}, u32[]{:S(2)}, u32[]{:S(2)}) collective-permute-start(f32[40,512]{1,0:T(8,128)S(1)} %get-tuple-element.202), channel_id=1, source_target_pairs={{1,2},{3,4},{5,6},{7,8},{9,10},{11,12},{13,14},{15,16},{17,18},{19... | collective-permute-start | bytes 245768 | tf_op jit(solution)/shard_map/ppermute | solution.py:493
  86.2 7.1 %collective-permute-start.30 = (f32[32,512]{1,0:T(8,128)S(1)}, f32[32,512]{1,0:T(8,128)S(1)}, u32[]{:S(2)}, u32[]{:S(2)}) collective-permute-start(f32[32,512]{1,0:T(8,128)S(1)} %get-tuple-element.201), channel_id=1, source_target_pairs={{0,1},{1,0},{2,3},{3,2},{4,5},{5,4},{6,7},{7,6},{8,9},{9,8},{10,11... | collective-permute-start | bytes 196616 | tf_op jit(solution)/shard_map/ppermute | solution.py:488
  94.5 4.9 %collective-permute-start.35 = (f32[72,128]{1,0:T(8,128)S(1)}, f32[72,128]{1,0:T(8,128)S(1)}, u32[]{:S(2)}, u32[]{:S(2)}) collective-permute-start(f32[72,128]{1,0:T(8,128)S(1)} %get-tuple-element.213.refs_1_), channel_id=1, source_target_pairs={{0,6},{1,7},{2,4},{3,5},{4,2},{5,3},{6,0},{7,1},{8,14},{9,15},{10,... | collective-permute-start | bytes 110600 | tf_op jit(solution)/shard_map/ppermute | solution.py:488
  102.0 5.6 %collective-permute-start.38 = (f32[40,128]{1,0:T(8,128)S(1)}, f32[40,128]{1,0:T(8,128)S(1)}, u32[]{:S(2)}, u32[]{:S(2)}) collective-permute-start(f32[40,128]{1,0:T(8,128)S(1)} %get-tuple-element.215.refs_1_), channel_id=1, source_target_pairs={{0,24},{1,25},{2,26},{3,27},{4,28},{5,29},{6,30},{7,31},{8,16},{9,... | collective-permute-start | bytes 61448 | tf_op jit(solution)/shard_map/ppermute | solution.py:488
  103.0 4.8 %collective-permute-start.37 = (f32[40,128]{1,0:T(8,128)S(1)}, f32[40,128]{1,0:T(8,128)S(1)}, u32[]{:S(2)}, u32[]{:S(2)}) collective-permute-start(f32[40,128]{1,0:T(8,128)S(1)} %get-tuple-element.215.refs_1_), channel_id=1, source_target_pairs={{0,16},{1,17},{2,18},{3,19},{4,20},{5,21},{6,22},{7,23},{8,24},{9,... | collective-permute-start | bytes 61448 | tf_op jit(solution)/shard_map/ppermute | solution.py:488
  (20 other events, 67.1 us)

commit v3 on v2

--- a/solution.py
+++ b/solution.py
@@ -153,14 +153,15 @@
         first_point = side * (leaves - 1) * LEAF
         sub_ref[side * LEAF : (side + 1) * LEAF] = lane_ref[:, first_point : first_point + LEAF].T
 
-        def one(part, carry):
+    def one(part, carry):
+        out_at = pl.ds(pl.multiple_of(part * CHUNK, CHUNK), CHUNK)
+        for side in range(2):
             row_at = pl.multiple_of(side * LEAF + part * CHUNK, CHUNK)
-            out_at = pl.ds(pl.multiple_of(part * CHUNK, CHUNK), CHUNK)
             values = matrix_rows(sub_ref[pl.ds(row_at, CHUNK)], lanes[side])
             high_ref[side, out_at], low_ref[side, out_at] = values
-            return carry
-
-        lax.fori_loop(0, LEAF // CHUNK, one, 0, unroll=4)
+        return carry
+
+    lax.fori_loop(0, LEAF // CHUNK, one, 0, unroll=4)
 
 
 def sides(core, field_ref):

time: 112 us -> 111 us (level)
  transfers between devices with their start and end apart: 40 -> 40, of which waited for: 17 -> 17; matrix products, arithmetic and copies ran while one was open for 0% -> 0% of each run, Pallas kernels for 24% -> 23%
where the time goes in v3:
time: 111 us
  starting transfers between devices  46.9 us (42%)
  Pallas kernels  41.9 us (38%)
  waiting for transfers between devices  20.4 us (18%)
    ppermute x36, starting transfers between devices, swap(): lax.ppermute(value, BOTH, [(source, source ^ mask) for source in range(de...  43.8 us
    pallas_call x35, Pallas kernels, call(): pl.pallas_call(body, out_shape=outs, in_specs=[whole(pltpu.SMEM)] * scala...  38.4 us
    ppermute x36, waiting for transfers between devices, swap(): lax.ppermute(value, BOTH, [(source, source ^ mask) for source in range(de...  20.4 us
    pallas_call x1, Pallas kernels, per_device(): pl.pallas_call(functools.partial(setup_kernel, groups[:1]), out_shape=[bf...  3.48 us
    ppermute x4, starting transfers between devices, far_halo(): lax.ppermute(other, BOTH, outward + [(target, source) for source, target...  3.05 us
  transfers between devices with their start and end apart: 40, of which 17 were waited for; matrix products, arithmetic and copies ran while one was open for 0% of the time, Pallas kernels for 23%

profile of v3, /device:TPU:0, one launch (start us, length us, event | category | flops | bytes accessed | tf_op | source)
XLA Modules:
  0.0 111.1 jit_solution(14662413907080054508)
XLA Ops:
  1.4 3.5 %shard_map.68 = (bf16[2,512,512]{2,1,0:T(8,128)(2,1)S(1)}, bf16[2,512,512]{2,1,0:T(8,128)(2,1)S(1)}, bf16[896,2048]{1,0:T(8,128)(2,1)S(1)}, bf16[896,2048]{1,0:T(8,128)(2,1)S(1)}, f32[8,2048]{1,0:T(8,128)S(1)}) custom-call(f32[3,2048]{1,0:T(4,128)S(1)} %copy-done.3, f32[7,128,2048]{2,1,0:T(8,128)} %basis_ref.1), custom_call_target="tpu_custom_call" | custom-call | flops 3000000000 | bytes 1048576 | tf_op jit(solution)/shard_map/pallas_call | solution.py:558
  4.9 2.3 %shard_map.70 = (f32[32,384]{1,0:T(8,128)S(1)}, f32[80,128]{1,0:T(8,128)S(1)}, f32[80,128]{1,0:T(8,128)S(1)}, f32[8,128]{1,0:T(8,128)S(1)}) custom-call(s32[1]{0:T(128)S(6)} %select_n.7.core_ref.refs_0_, f32[32,2048]{1,0:T(8,128)S(1)} %copy-done, bf16[896,2048]{1,0:T(8,128)(2,1)S(1)} %get-tuple-element.112.high_ref.refs_1_, ...), custom_call_target="tpu_custom_call" | custom-call | flops 3000000000 | bytes 1048576 | tf_op jit(solution)/shard_map/pallas_call | solution.py:83
  9.1 5.4 %collective-permute-start.5 = (f32[72,128]{1,0:T(8,128)S(1)}, f32[72,128]{1,0:T(8,128)S(1)}, u32[]{:S(2)}, u32[]{:S(2)}) collective-permute-start(f32[72,128]{1,0:T(8,128)S(1)} %get-tuple-element.119.refs_1_), channel_id=1, source_target_pairs={{0,6},{1,7},{2,4},{3,5},{4,2},{5,3},{6,0},{7,1},{8,14},{9,15},{10,... | collective-permute-start | bytes 110600 | tf_op jit(solution)/shard_map/ppermute | solution.py:489
  15.9 5.6 %shard_map.72 = (bf16[5,512,512]{2,1,0:T(8,128)(2,1)S(1)}, bf16[5,512,512]{2,1,0:T(8,128)(2,1)S(1)}) custom-call(f32[8,2048]{1,0:T(8,128)S(1)} %get-tuple-element.131.lane_ref.refs_0_), custom_call_target="tpu_custom_call" | custom-call | flops 6000000000 | bytes 1048576 | tf_op jit(solution)/shard_map/pallas_call | solution.py:83
  21.5 5.1 %collective-permute-start.8 = (f32[40,128]{1,0:T(8,128)S(1)}, f32[40,128]{1,0:T(8,128)S(1)}, u32[]{:S(2)}, u32[]{:S(2)}) collective-permute-start(f32[40,128]{1,0:T(8,128)S(1)} %get-tuple-element.130.refs_1_), channel_id=1, source_target_pairs={{0,24},{1,25},{2,26},{3,27},{4,28},{5,29},{6,30},{7,31},{8,16},{9,... | collective-permute-start | bytes 61448 | tf_op jit(solution)/shard_map/ppermute | solution.py:489
  29.7 2.2 %shard_map.74 = (bf16[2,512,512]{2,1,0:T(8,128)(2,1)S(1)}, bf16[2,512,512]{2,1,0:T(8,128)(2,1)S(1)}) custom-call(s32[1]{0:T(128)S(6)} %select_n.7.core_ref.refs_0_, f32[8,2048]{1,0:T(8,128)S(1)} %get-tuple-element.131.lane_ref.refs_0_, f32[40,512]{1,0:T(8,128)S(1)} %collective-permute-done.1.refs_1_.refs_2_, f32[40,512]{1,0:T(8,128)S(1)} %collective-permute-done.2.refs_2_.refs_3_), custom_call_target="tpu_custom_call" | custom-call | flops 3000000000 | bytes 1048576 | tf_op jit(solution)/shard_map/pallas_call | solution.py:83
  35.5 1.5 %collective-permute-start.10 = (f32[32,512]{1,0:T(8,128)S(1)}, f32[32,512]{1,0:T(8,128)S(1)}, u32[]{:S(2)}, u32[]{:S(2)}) collective-permute-start(f32[32,512]{1,0:T(8,128)S(1)} %get-tuple-element.150), channel_id=1, source_target_pairs={{0,1},{1,0},{2,3},{3,2},{4,5},{5,4},{6,7},{7,6},{8,9},{9,8},{10,11... | collective-permute-start | bytes 196616 | tf_op jit(solution)/shard_map/ppermute | solution.py:489
  36.9 2.3 %shard_map.82 = (f32[32,384]{1,0:T(8,128)S(1)}, f32[80,128]{1,0:T(8,128)S(1)}, f32[80,128]{1,0:T(8,128)S(1)}) custom-call(s32[1]{0:T(128)S(6)} %select_n.7.core_ref.refs_0_, f32[32,2048]{1,0:T(8,128)S(1)} %get-tuple-element.152.field_ref.refs_9_.refs_11_.refs_8_.refs_10_, bf16[896,2048]{1,0:T(8,128)(2,1)S(1)} %get-tuple-element.112.high_ref.refs_1_, ...), custom_call_target="tpu_custom_call" | custom-call | tf_op jit(solution)/shard_map/pallas_call | solution.py:83
  42.9 3.7 %collective-permute-start.15 = (f32[72,128]{1,0:T(8,128)S(1)}, f32[72,128]{1,0:T(8,128)S(1)}, u32[]{:S(2)}, u32[]{:S(2)}) collective-permute-start(f32[72,128]{1,0:T(8,128)S(1)} %get-tuple-element.158.refs_1_), channel_id=1, source_target_pairs={{0,6},{1,7},{2,4},{3,5},{4,2},{5,3},{6,0},{7,1},{8,14},{9,15},{10,... | collective-permute-start | bytes 110600 | tf_op jit(solution)/shard_map/ppermute | solution.py:489
  47.2 1.5 %collective-permute-done.15.refs_4_ = f32[72,128]{1,0:T(8,128)S(1)} collective-permute-done((f32[72,128]{1,0:T(8,128)S(1)}, f32[72,128]{1,0:T(8,128)S(1)}, u32[]{:S(2)}, u32[]{:S(2)}) %collective-permute-start.15) | collective-permute-done | bytes 36896 | tf_op jit(solution)/shard_map/ppermute | solution.py:489
  48.7 1.8 %collective-permute-done.14.refs_3_ = f32[72,128]{1,0:T(8,128)S(1)} collective-permute-done((f32[72,128]{1,0:T(8,128)S(1)}, f32[72,128]{1,0:T(8,128)S(1)}, u32[]{:S(2)}, u32[]{:S(2)}) %collective-permute-start.14) | collective-permute-done | bytes 36896 | tf_op jit(solution)/shard_map/ppermute | solution.py:489
  50.8 3.6 %collective-permute-start.18 = (f32[40,128]{1,0:T(8,128)S(1)}, f32[40,128]{1,0:T(8,128)S(1)}, u32[]{:S(2)}, u32[]{:S(2)}) collective-permute-start(f32[40,128]{1,0:T(8,128)S(1)} %get-tuple-element.160.refs_1_), channel_id=1, source_target_pairs={{0,24},{1,25},{2,26},{3,27},{4,28},{5,29},{6,30},{7,31},{8,16},{9,... | collective-permute-start | bytes 61448 | tf_op jit(solution)/shard_map/ppermute | solution.py:489
  56.5 2.7 %collective-permute-done.17.refs_3_ = f32[40,128]{1,0:T(8,128)S(1)} collective-permute-done((f32[40,128]{1,0:T(8,128)S(1)}, f32[40,128]{1,0:T(8,128)S(1)}, u32[]{:S(2)}, u32[]{:S(2)}) %collective-permute-start.17) | collective-permute-done | bytes 20512 | tf_op jit(solution)/shard_map/ppermute | solution.py:489
  62.1 2.3 %shard_map.88 = (f32[32,384]{1,0:T(8,128)S(1)}, f32[80,128]{1,0:T(8,128)S(1)}, f32[80,128]{1,0:T(8,128)S(1)}, f32[8,128]{1,0:T(8,128)S(1)}) custom-call(s32[1]{0:T(128)S(6)} %select_n.7.core_ref.refs_0_, f32[32,2048]{1,0:T(8,128)S(1)} %get-tuple-element.174.field_ref.refs_7_.refs_8_, bf16[896,2048]{1,0:T(8,128)(2,1)S(1)} %get-tuple-element.112.high_ref.refs_1_, ...), custom_call_target="tpu_custom_call" | custom-call | tf_op jit(solution)/shard_map/pallas_call | solution.py:83
  65.3 1.8 %collective-permute-start.27 = (f32[32,512]{1,0:T(8,128)S(1)}, f32[32,512]{1,0:T(8,128)S(1)}, u32[]{:S(2)}, u32[]{:S(2)}) collective-permute-start(f32[32,512]{1,0:T(8,128)S(1)} %get-tuple-element.179), channel_id=1, source_target_pairs={{0,1},{1,0},{2,3},{3,2},{4,5},{5,4},{6,7},{7,6},{8,9},{9,8},{10,11... | collective-permute-start | bytes 196616 | tf_op jit(solution)/shard_map/ppermute | solution.py:489
  67.1 1.9 %collective-permute-start.23 = (f32[72,128]{1,0:T(8,128)S(1)}, f32[72,128]{1,0:T(8,128)S(1)}, u32[]{:S(2)}, u32[]{:S(2)}) collective-permute-start(f32[72,128]{1,0:T(8,128)S(1)} %get-tuple-element.173.refs_1_), channel_id=1, source_target_pairs={{0,6},{1,7},{2,4},{3,5},{4,2},{5,3},{6,0},{7,1},{8,14},{9,15},{10,... | collective-permute-start | bytes 110600 | tf_op jit(solution)/shard_map/ppermute | solution.py:489
  74.4 2.7 %collective-permute-start.26 = (f32[40,128]{1,0:T(8,128)S(1)}, f32[40,128]{1,0:T(8,128)S(1)}, u32[]{:S(2)}, u32[]{:S(2)}) collective-permute-start(f32[40,128]{1,0:T(8,128)S(1)} %get-tuple-element.178.refs_1_), channel_id=1, source_target_pairs={{0,24},{1,25},{2,26},{3,27},{4,28},{5,29},{6,30},{7,31},{8,16},{9,... | collective-permute-start | bytes 61448 | tf_op jit(solution)/shard_map/ppermute | solution.py:489
  77.2 1.6 %collective-permute-start.24 = (f32[40,128]{1,0:T(8,128)S(1)}, f32[40,128]{1,0:T(8,128)S(1)}, u32[]{:S(2)}, u32[]{:S(2)}) collective-permute-start(f32[40,128]{1,0:T(8,128)S(1)} %get-tuple-element.178.refs_1_), channel_id=1, source_target_pairs={{0,8},{1,9},{2,10},{3,11},{4,12},{5,13},{6,14},{7,15},{8,0},{9,1},... | collective-permute-start | bytes 61448 | tf_op jit(solution)/shard_map/ppermute | solution.py:489
  80.1 1.7 %collective-permute-done.25.refs_3_ = f32[40,128]{1,0:T(8,128)S(1)} collective-permute-done((f32[40,128]{1,0:T(8,128)S(1)}, f32[40,128]{1,0:T(8,128)S(1)}, u32[]{:S(2)}, u32[]{:S(2)}) %collective-permute-start.25) | collective-permute-done | bytes 20512 | tf_op jit(solution)/shard_map/ppermute | solution.py:489
  85.4 2.3 %collective-permute-start.30 = (f32[32,512]{1,0:T(8,128)S(1)}, f32[32,512]{1,0:T(8,128)S(1)}, u32[]{:S(2)}, u32[]{:S(2)}) collective-permute-start(f32[32,512]{1,0:T(8,128)S(1)} %get-tuple-element.201), channel_id=1, source_target_pairs={{0,1},{1,0},{2,3},{3,2},{4,5},{5,4},{6,7},{7,6},{8,9},{9,8},{10,11... | collective-permute-start | bytes 196616 | tf_op jit(solution)/shard_map/ppermute | solution.py:489
  87.8 2.3 %shard_map.98 = (f32[32,384]{1,0:T(8,128)S(1)}, f32[80,128]{1,0:T(8,128)S(1)}, f32[80,128]{1,0:T(8,128)S(1)}) custom-call(s32[1]{0:T(128)S(6)} %select_n.7.core_ref.refs_0_, f32[32,2048]{1,0:T(8,128)S(1)} %get-tuple-element.203.field_ref.refs_9_.refs_10_, bf16[896,2048]{1,0:T(8,128)(2,1)S(1)} %get-tuple-element.112.high_ref.refs_1_, ...), custom_call_target="tpu_custom_call" | custom-call | tf_op jit(solution)/shard_map/pallas_call | solution.py:83
  93.7 2.3 %collective-permute-start.35 = (f32[72,128]{1,0:T(8,128)S(1)}, f32[72,128]{1,0:T(8,128)S(1)}, u32[]{:S(2)}, u32[]{:S(2)}) collective-permute-start(f32[72,128]{1,0:T(8,128)S(1)} %get-tuple-element.213.refs_1_), channel_id=1, source_target_pairs={{0,6},{1,7},{2,4},{3,5},{4,2},{5,3},{6,0},{7,1},{8,14},{9,15},{10,... | collective-permute-start | bytes 110600 | tf_op jit(solution)/shard_map/ppermute | solution.py:489
  103.5 2.2 %collective-permute-start.36 = (f32[40,128]{1,0:T(8,128)S(1)}, f32[40,128]{1,0:T(8,128)S(1)}, u32[]{:S(2)}, u32[]{:S(2)}) collective-permute-start(f32[40,128]{1,0:T(8,128)S(1)} %get-tuple-element.215.refs_1_), channel_id=1, source_target_pairs={{0,8},{1,9},{2,10},{3,11},{4,12},{5,13},{6,14},{7,15},{8,0},{9,1},... | collective-permute-start | bytes 61448 | tf_op jit(solution)/shard_map/ppermute | solution.py:489
  108.9 2.2 %shard_map.103 = (f32[32,2048]{1,0:T(8,128)}, f32[32,2048]{1,0:T(8,128)}) custom-call(s32[1]{0:T(128)S(6)} %select_n.7.core_ref.refs_0_, bf16[896,2048]{1,0:T(8,128)(2,1)S(1)} %get-tuple-element.112.high_ref.refs_1_, bf16[896,2048]{1,0:T(8,128)(2,1)S(1)} %get-tuple-element.113.low_ref.refs_2_, f32[32,2048]{1,0:T(8,128)S(1)} %get-tuple-element.208.refs_3_, ...), custom_call_target="tpu_custom_call" | custom-call | flops 1500000000 | bytes 1048576 | tf_op jit(solution)/shard_map/pallas_call | solution.py:83
  (100 shorter events, 45.5 us)
Async XLA Ops:
  8.4 21.3 %collective-permute-start.2 = (f32[40,512]{1,0:T(8,128)S(1)}, f32[40,512]{1,0:T(8,128)S(1)}, u32[]{:S(2)}, u32[]{:S(2)}) collective-permute-start(f32[40,512]{1,0:T(8,128)S(1)} %get-tuple-element.123), channel_id=1, source_target_pairs={{1,2},{3,4},{5,6},{7,8},{9,10},{11,12},{13,14},{15,16},{17,18},{19... | collective-permute-start | bytes 245768 | tf_op jit(solution)/shard_map/ppermute | solution.py:494
  9.1 12.4 %collective-permute-start.5 = (f32[72,128]{1,0:T(8,128)S(1)}, f32[72,128]{1,0:T(8,128)S(1)}, u32[]{:S(2)}, u32[]{:S(2)}) collective-permute-start(f32[72,128]{1,0:T(8,128)S(1)} %get-tuple-element.119.refs_1_), channel_id=1, source_target_pairs={{0,6},{1,7},{2,4},{3,5},{4,2},{5,3},{6,0},{7,1},{8,14},{9,15},{10,... | collective-permute-start | bytes 110600 | tf_op jit(solution)/shard_map/ppermute | solution.py:489
  14.5 7.0 %collective-permute-start.4 = (f32[72,128]{1,0:T(8,128)S(1)}, f32[72,128]{1,0:T(8,128)S(1)}, u32[]{:S(2)}, u32[]{:S(2)}) collective-permute-start(f32[72,128]{1,0:T(8,128)S(1)} %get-tuple-element.119.refs_1_), channel_id=1, source_target_pairs={{0,4},{1,5},{2,6},{3,7},{4,0},{5,1},{6,2},{7,3},{8,12},{9,13},{10,... | collective-permute-start | bytes 110600 | tf_op jit(solution)/shard_map/ppermute | solution.py:489
  14.5 7.0 %collective-permute-start.3 = (f32[72,128]{1,0:T(8,128)S(1)}, f32[72,128]{1,0:T(8,128)S(1)}, u32[]{:S(2)}, u32[]{:S(2)}) collective-permute-start(f32[72,128]{1,0:T(8,128)S(1)} %get-tuple-element.119.refs_1_), channel_id=1, source_target_pairs={{0,2},{1,3},{2,0},{3,1},{4,6},{5,7},{6,4},{7,5},{8,10},{9,11},{10,... | collective-permute-start | bytes 110600 | tf_op jit(solution)/shard_map/ppermute | solution.py:489
  15.9 13.8 %collective-permute-start.1 = (f32[40,512]{1,0:T(8,128)S(1)}, f32[40,512]{1,0:T(8,128)S(1)}, u32[]{:S(2)}, u32[]{:S(2)}) collective-permute-start(f32[40,512]{1,0:T(8,128)S(1)} %get-tuple-element.121), channel_id=1, source_target_pairs={{0,1},{1,0},{2,3},{3,2},{4,5},{5,4},{6,7},{7,6},{8,9},{9,8},{10,11... | collective-permute-start | bytes 245768 | tf_op jit(solution)/shard_map/ppermute | solution.py:489
  21.5 10.3 %collective-permute-start.8 = (f32[40,128]{1,0:T(8,128)S(1)}, f32[40,128]{1,0:T(8,128)S(1)}, u32[]{:S(2)}, u32[]{:S(2)}) collective-permute-start(f32[40,128]{1,0:T(8,128)S(1)} %get-tuple-element.130.refs_1_), channel_id=1, source_target_pairs={{0,24},{1,25},{2,26},{3,27},{4,28},{5,29},{6,30},{7,31},{8,16},{9,... | collective-permute-start | bytes 61448 | tf_op jit(solution)/shard_map/ppermute | solution.py:489
  26.6 5.3 %collective-permute-start.7 = (f32[40,128]{1,0:T(8,128)S(1)}, f32[40,128]{1,0:T(8,128)S(1)}, u32[]{:S(2)}, u32[]{:S(2)}) collective-permute-start(f32[40,128]{1,0:T(8,128)S(1)} %get-tuple-element.130.refs_1_), channel_id=1, source_target_pairs={{0,16},{1,17},{2,18},{3,19},{4,20},{5,21},{6,22},{7,23},{8,24},{9,... | collective-permute-start | bytes 61448 | tf_op jit(solution)/shard_map/ppermute | solution.py:489
  26.6 5.3 %collective-permute-start.6 = (f32[40,128]{1,0:T(8,128)S(1)}, f32[40,128]{1,0:T(8,128)S(1)}, u32[]{:S(2)}, u32[]{:S(2)}) collective-permute-start(f32[40,128]{1,0:T(8,128)S(1)} %get-tuple-element.130.refs_1_), channel_id=1, source_target_pairs={{0,8},{1,9},{2,10},{3,11},{4,12},{5,13},{6,14},{7,15},{8,0},{9,1},... | collective-permute-start | bytes 61448 | tf_op jit(solution)/shard_map/ppermute | solution.py:489
  34.6 7.1 %collective-permute-start.11 = (f32[40,512]{1,0:T(8,128)S(1)}, f32[40,512]{1,0:T(8,128)S(1)}, u32[]{:S(2)}, u32[]{:S(2)}) collective-permute-start(f32[40,512]{1,0:T(8,128)S(1)} %get-tuple-element.151), channel_id=1, source_target_pairs={{1,2},{3,4},{5,6},{7,8},{9,10},{11,12},{13,14},{15,16},{17,18},{19... | collective-permute-start | bytes 245768 | tf_op jit(solution)/shard_map/ppermute | solution.py:494
  35.5 6.2 %collective-permute-start.10 = (f32[32,512]{1,0:T(8,128)S(1)}, f32[32,512]{1,0:T(8,128)S(1)}, u32[]{:S(2)}, u32[]{:S(2)}) collective-permute-start(f32[32,512]{1,0:T(8,128)S(1)} %get-tuple-element.150), channel_id=1, source_target_pairs={{0,1},{1,0},{2,3},{3,2},{4,5},{5,4},{6,7},{7,6},{8,9},{9,8},{10,11... | collective-permute-start | bytes 196616 | tf_op jit(solution)/shard_map/ppermute | solution.py:489
  42.9 5.9 %collective-permute-start.15 = (f32[72,128]{1,0:T(8,128)S(1)}, f32[72,128]{1,0:T(8,128)S(1)}, u32[]{:S(2)}, u32[]{:S(2)}) collective-permute-start(f32[72,128]{1,0:T(8,128)S(1)} %get-tuple-element.158.refs_1_), channel_id=1, source_target_pairs={{0,6},{1,7},{2,4},{3,5},{4,2},{5,3},{6,0},{7,1},{8,14},{9,15},{10,... | collective-permute-start | bytes 110600 | tf_op jit(solution)/shard_map/ppermute | solution.py:489
  50.8 5.7 %collective-permute-start.18 = (f32[40,128]{1,0:T(8,128)S(1)}, f32[40,128]{1,0:T(8,128)S(1)}, u32[]{:S(2)}, u32[]{:S(2)}) collective-permute-start(f32[40,128]{1,0:T(8,128)S(1)} %get-tuple-element.160.refs_1_), channel_id=1, source_target_pairs={{0,24},{1,25},{2,26},{3,27},{4,28},{5,29},{6,30},{7,31},{8,16},{9,... | collective-permute-start | bytes 61448 | tf_op jit(solution)/shard_map/ppermute | solution.py:489
  54.4 4.7 %collective-permute-start.17 = (f32[40,128]{1,0:T(8,128)S(1)}, f32[40,128]{1,0:T(8,128)S(1)}, u32[]{:S(2)}, u32[]{:S(2)}) collective-permute-start(f32[40,128]{1,0:T(8,128)S(1)} %get-tuple-element.160.refs_1_), channel_id=1, source_target_pairs={{0,16},{1,17},{2,18},{3,19},{4,20},{5,21},{6,22},{7,23},{8,24},{9,... | collective-permute-start | bytes 61448 | tf_op jit(solution)/shard_map/ppermute | solution.py:489
  54.5 4.7 %collective-permute-start.16 = (f32[40,128]{1,0:T(8,128)S(1)}, f32[40,128]{1,0:T(8,128)S(1)}, u32[]{:S(2)}, u32[]{:S(2)}) collective-permute-start(f32[40,128]{1,0:T(8,128)S(1)} %get-tuple-element.160.refs_1_), channel_id=1, source_target_pairs={{0,8},{1,9},{2,10},{3,11},{4,12},{5,13},{6,14},{7,15},{8,0},{9,1},... | collective-permute-start | bytes 61448 | tf_op jit(solution)/shard_map/ppermute | solution.py:489
  64.6 14.2 %collective-permute-start.28 = (f32[40,512]{1,0:T(8,128)S(1)}, f32[40,512]{1,0:T(8,128)S(1)}, u32[]{:S(2)}, u32[]{:S(2)}) collective-permute-start(f32[40,512]{1,0:T(8,128)S(1)} %get-tuple-element.180), channel_id=1, source_target_pairs={{1,2},{3,4},{5,6},{7,8},{9,10},{11,12},{13,14},{15,16},{17,18},{19... | collective-permute-start | bytes 245768 | tf_op jit(solution)/shard_map/ppermute | solution.py:494
  65.3 13.6 %collective-permute-start.27 = (f32[32,512]{1,0:T(8,128)S(1)}, f32[32,512]{1,0:T(8,128)S(1)}, u32[]{:S(2)}, u32[]{:S(2)}) collective-permute-start(f32[32,512]{1,0:T(8,128)S(1)} %get-tuple-element.179), channel_id=1, source_target_pairs={{0,1},{1,0},{2,3},{3,2},{4,5},{5,4},{6,7},{7,6},{8,9},{9,8},{10,11... | collective-permute-start | bytes 196616 | tf_op jit(solution)/shard_map/ppermute | solution.py:489
  67.1 6.0 %collective-permute-start.23 = (f32[72,128]{1,0:T(8,128)S(1)}, f32[72,128]{1,0:T(8,128)S(1)}, u32[]{:S(2)}, u32[]{:S(2)}) collective-permute-start(f32[72,128]{1,0:T(8,128)S(1)} %get-tuple-element.173.refs_1_), channel_id=1, source_target_pairs={{0,6},{1,7},{2,4},{3,5},{4,2},{5,3},{6,0},{7,1},{8,14},{9,15},{10,... | collective-permute-start | bytes 110600 | tf_op jit(solution)/shard_map/ppermute | solution.py:489
  74.4 5.6 %collective-permute-start.26 = (f32[40,128]{1,0:T(8,128)S(1)}, f32[40,128]{1,0:T(8,128)S(1)}, u32[]{:S(2)}, u32[]{:S(2)}) collective-permute-start(f32[40,128]{1,0:T(8,128)S(1)} %get-tuple-element.178.refs_1_), channel_id=1, source_target_pairs={{0,24},{1,25},{2,26},{3,27},{4,28},{5,29},{6,30},{7,31},{8,16},{9,... | collective-permute-start | bytes 61448 | tf_op jit(solution)/shard_map/ppermute | solution.py:489
  77.1 4.7 %collective-permute-start.25 = (f32[40,128]{1,0:T(8,128)S(1)}, f32[40,128]{1,0:T(8,128)S(1)}, u32[]{:S(2)}, u32[]{:S(2)}) collective-permute-start(f32[40,128]{1,0:T(8,128)S(1)} %get-tuple-element.178.refs_1_), channel_id=1, source_target_pairs={{0,16},{1,17},{2,18},{3,19},{4,20},{5,21},{6,22},{7,23},{8,24},{9,... | collective-permute-start | bytes 61448 | tf_op jit(solution)/shard_map/ppermute | solution.py:489
  84.5 8.0 %collective-permute-start.31 = (f32[40,512]{1,0:T(8,128)S(1)}, f32[40,512]{1,0:T(8,128)S(1)}, u32[]{:S(2)}, u32[]{:S(2)}) collective-permute-start(f32[40,512]{1,0:T(8,128)S(1)} %get-tuple-element.202), channel_id=1, source_target_pairs={{1,2},{3,4},{5,6},{7,8},{9,10},{11,12},{13,14},{15,16},{17,18},{19... | collective-permute-start | bytes 245768 | tf_op jit(solution)/shard_map/ppermute | solution.py:494
  85.4 7.1 %collective-permute-start.30 = (f32[32,512]{1,0:T(8,128)S(1)}, f32[32,512]{1,0:T(8,128)S(1)}, u32[]{:S(2)}, u32[]{:S(2)}) collective-permute-start(f32[32,512]{1,0:T(8,128)S(1)} %get-tuple-element.201), channel_id=1, source_target_pairs={{0,1},{1,0},{2,3},{3,2},{4,5},{5,4},{6,7},{7,6},{8,9},{9,8},{10,11... | collective-permute-start | bytes 196616 | tf_op jit(solution)/shard_map/ppermute | solution.py:489
  93.7 4.9 %collective-permute-start.35 = (f32[72,128]{1,0:T(8,128)S(1)}, f32[72,128]{1,0:T(8,128)S(1)}, u32[]{:S(2)}, u32[]{:S(2)}) collective-permute-start(f32[72,128]{1,0:T(8,128)S(1)} %get-tuple-element.213.refs_1_), channel_id=1, source_target_pairs={{0,6},{1,7},{2,4},{3,5},{4,2},{5,3},{6,0},{7,1},{8,14},{9,15},{10,... | collective-permute-start | bytes 110600 | tf_op jit(solution)/shard_map/ppermute | solution.py:489
  101.2 5.6 %collective-permute-start.38 = (f32[40,128]{1,0:T(8,128)S(1)}, f32[40,128]{1,0:T(8,128)S(1)}, u32[]{:S(2)}, u32[]{:S(2)}) collective-permute-start(f32[40,128]{1,0:T(8,128)S(1)} %get-tuple-element.215.refs_1_), channel_id=1, source_target_pairs={{0,24},{1,25},{2,26},{3,27},{4,28},{5,29},{6,30},{7,31},{8,16},{9,... | collective-permute-start | bytes 61448 | tf_op jit(solution)/shard_map/ppermute | solution.py:489
  102.2 4.8 %collective-permute-start.37 = (f32[40,128]{1,0:T(8,128)S(1)}, f32[40,128]{1,0:T(8,128)S(1)}, u32[]{:S(2)}, u32[]{:S(2)}) collective-permute-start(f32[40,128]{1,0:T(8,128)S(1)} %get-tuple-element.215.refs_1_), channel_id=1, source_target_pairs={{0,16},{1,17},{2,18},{3,19},{4,20},{5,21},{6,22},{7,23},{8,24},{9,... | collective-permute-start | bytes 61448 | tf_op jit(solution)/shard_map/ppermute | solution.py:489
  (20 other events, 67.1 us)
